TPU v7x, 32 devices: a whole 2x2x4 slice. The times are simulated.
32 devices in a mesh: depth: 4 (over y, core), az: 8 (over z, x).
Axes of the slice: x: 2, y: 2, z: 4, core: 2. Of those that a mesh axis runs over, the one named last changes fastest.
Arguments:
- pressure_field: float32 [2, 2048, 4096], P(None, 'depth', 'az'), may hold values from -6 to 6
- block_inverses: float32 [2, 8, 16, 128, 128], P(None, None, 'depth'), may hold values from -1.25 to 1.25, as said below
- lower_spikes: float32 [2, 8, 16, 128], P(None, None, 'depth'), may hold values from -1 to 1, as said below
- upper_spikes: float32 [2, 8, 16, 128], P(None, None, 'depth'), may hold values from -1 to 1, as said below
- pade_weights: float32 [2, 8], replicated, may hold values from -0.08 to 0.08
- layer_wavenumber: float32 [2, 5], replicated, may hold values from -0.4 to 0.4
- layer_index: int32 [16], P('depth'), may hold values from 0 to 4
- depth_coupling: float32 [2048], P('depth'), may hold values from 0.05 to 1
- attenuation: float32 [5, 6], replicated, may hold values from 0.02 to 0.4
- sediment_type: int32 [4096], P('az'), may hold values from 0 to 5
Outputs:
- final_field: float32 [2, 2048, 4096], P(None, 'depth', 'az')
Inputs may be any that keep to these rules, and one draw needn't show every extreme that they name: `block_inverses`: complex blocks whose diagonal entries have real parts between 0.75 and 1.25, every other entry smaller in magnitude than the diagonal ones. `lower_spikes`: the last entry of each spike has magnitude below 1. `upper_spikes`: the first entry of each spike has magnitude below 1.
All inputs are finite; a program needn't handle non-finite values.
Results may differ from a plain program's by a relative error of at most 0.0001.
Values sent between devices are 32-bit elements; how exact they have to be, the bound alone decides.
A program may use at most 128 MiB of HBM per device.

v0:
```python
import math

import jax
import jax.numpy as jnp
from jax import lax
from jax.sharding import PartitionSpec as P

AZ_ROWS = 32
AZ_COLS = 128
STEPS = 2


FULL_PRECISION = lax.Precision.HIGHEST


def entering_2(value, axis, combine, identity, reverse):
    size, index = (lax.axis_size(axis), lax.axis_index(axis))
    everything = jax.tree.map(lambda part: lax.all_gather(part, axis), value)
    start = jax.tree.map(
        lambda part, zero: jnp.broadcast_to(jnp.asarray(zero, part.dtype), part.shape),
        value,
        identity,
    )

    def hop(k, before):
        at = size - 1 - k if reverse else k
        reached = at > index if reverse else at < index
        new = combine(before, jax.tree.map(lambda part: part[at], everything))
        return jax.tree.map(lambda a, b: jnp.where(reached, a, b), new, before)

    return lax.fori_loop(0, size, hop, start)


def extended(cells, sides, width):
    for axis, dim in sides:
        count = lax.axis_size(axis)
        ends = count - 1
        head = lax.slice_in_dim(cells, 0, width, axis=dim)
        tail = lax.slice_in_dim(cells, cells.shape[dim] - width, cells.shape[dim], axis=dim)
        cells = jnp.concatenate(
            [
                lax.ppermute(tail, axis, [(i, (i + 1) % count) for i in range(ends)]),
                cells,
                lax.ppermute(head, axis, [((i + 1) % count, i) for i in range(ends)]),
            ],
            axis=dim,
        )
    return cells


def complex_einsum(formula, left_re, left_im, right_re, right_im):
    real_part = jnp.einsum(formula, left_re, right_re, precision=FULL_PRECISION) - jnp.einsum(
        formula, left_im, right_im, precision=FULL_PRECISION
    )
    imag_part = jnp.einsum(formula, left_re, right_im, precision=FULL_PRECISION) + jnp.einsum(
        formula, left_im, right_re, precision=FULL_PRECISION
    )
    return (real_part, imag_part)


def compose(earlier, later):
    a_re, a_im, b_re, b_im = earlier
    c_re, c_im, d_re, d_im = later
    return (
        c_re * a_re - c_im * a_im,
        c_re * a_im + c_im * a_re,
        c_re[:, None] * b_re - c_im[:, None] * b_im + d_re,
        c_re[:, None] * b_im + c_im[:, None] * b_re + d_im,
    )


def apply_map(factor_re, factor_im, offset_re, offset_im, carried):
    return (
        factor_re[:, None] * carried[0] - factor_im[:, None] * carried[1] + offset_re,
        factor_re[:, None] * carried[1] + factor_im[:, None] * carried[0] + offset_im,
    )


def neutral_map(block_map):
    return (
        jnp.ones_like(block_map[0]),
        jnp.zeros_like(block_map[1]),
        jnp.zeros_like(block_map[2]),
        jnp.zeros_like(block_map[3]),
    )


def block_maps(factor_re, factor_im, offset_re, offset_im, ordering):
    combined = (
        jnp.ones_like(factor_re[:, 0]),
        jnp.zeros_like(factor_im[:, 0]),
        jnp.zeros_like(offset_re[:, 0]),
        jnp.zeros_like(offset_im[:, 0]),
    )
    for block_pos in ordering:
        combined = compose(
            combined,
            (
                factor_re[:, block_pos],
                factor_im[:, block_pos],
                offset_re[:, block_pos],
                offset_im[:, block_pos],
            ),
        )
    return combined


def block_carries(start_value, factor_re, factor_im, offset_re, offset_im, ordering):
    carried = start_value
    entering = [None] * factor_re.shape[1]
    for block_pos in ordering:
        entering[block_pos] = carried
        carried = apply_map(
            factor_re[:, block_pos],
            factor_im[:, block_pos],
            offset_re[:, block_pos],
            offset_im[:, block_pos],
            carried,
        )
    return (
        jnp.stack([entry[0] for entry in entering], axis=1),
        jnp.stack([entry[1] for entry in entering], axis=1),
    )


def link_forward(block_map):
    prefix = entering_2(
        (block_map[0], block_map[1], block_map[2], block_map[3]),
        "depth",
        compose,
        neutral_map(block_map),
        False,
    )
    result_value = (prefix[2], prefix[3])
    return result_value


def link_backward(block_map):
    prefix = entering_2(
        (block_map[0], block_map[1], block_map[2], block_map[3]),
        "depth",
        compose,
        neutral_map(block_map),
        True,
    )
    result_value = (prefix[2], prefix[3])
    return result_value


def advance(field_part, operator_part, block_inverses, lower_spikes, upper_spikes, pade_weights):
    depth_rows = field_part.shape[1]
    az_count = field_part.shape[2]
    block_count = block_inverses.shape[2]
    block_rows = block_inverses.shape[3]
    shaped = operator_part.reshape(2, block_count, block_rows, az_count)
    solved_re, solved_im = complex_einsum(
        "tbij,bjn->tbin", block_inverses[0], block_inverses[1], shaped[0], shaped[1]
    )
    lower_re = lower_spikes[0]
    lower_im = lower_spikes[1]
    upward = list(range(block_count))
    factor_re = -lower_re[:, :, -1]
    factor_im = -lower_im[:, :, -1]
    forward_map = block_maps(factor_re, factor_im, solved_re[:, :, -1], solved_im[:, :, -1], upward)
    enter_re, enter_im = block_carries(
        link_forward(forward_map),
        factor_re,
        factor_im,
        solved_re[:, :, -1],
        solved_im[:, :, -1],
        upward,
    )
    swept_re = solved_re - (
        lower_re[..., None] * enter_re[:, :, None] - lower_im[..., None] * enter_im[:, :, None]
    )
    swept_im = solved_im - (
        lower_re[..., None] * enter_im[:, :, None] + lower_im[..., None] * enter_re[:, :, None]
    )
    upper_re = upper_spikes[0]
    upper_im = upper_spikes[1]
    downward = list(reversed(range(block_count)))
    back_factor_re = -upper_re[:, :, 0]
    back_factor_im = -upper_im[:, :, 0]
    backward_map = block_maps(
        back_factor_re, back_factor_im, swept_re[:, :, 0], swept_im[:, :, 0], downward
    )
    below_re, below_im = block_carries(
        link_backward(backward_map),
        back_factor_re,
        back_factor_im,
        swept_re[:, :, 0],
        swept_im[:, :, 0],
        downward,
    )
    final_re = swept_re - (
        upper_re[..., None] * below_re[:, :, None] - upper_im[..., None] * below_im[:, :, None]
    )
    final_im = swept_im - (
        upper_re[..., None] * below_im[:, :, None] + upper_im[..., None] * below_re[:, :, None]
    )
    incr_re = jnp.einsum(
        "t,tbin->bin", pade_weights[0], final_re, precision=FULL_PRECISION
    ) - jnp.einsum("t,tbin->bin", pade_weights[1], final_im, precision=FULL_PRECISION)
    incr_im = jnp.einsum(
        "t,tbin->bin", pade_weights[0], final_im, precision=FULL_PRECISION
    ) + jnp.einsum("t,tbin->bin", pade_weights[1], final_re, precision=FULL_PRECISION)
    return field_part + jnp.stack([incr_re, incr_im]).reshape(2, depth_rows, az_count)


def dft_table(length, sign_factor):
    product = jnp.arange(length)[:, None] * jnp.arange(length)[None, :] % length
    angles = 2.0 * math.pi / length * product.astype(jnp.float32)
    return (jnp.cos(angles), sign_factor * jnp.sin(angles))


def couple_azimuths(columns, coupling_rows):
    row_count = columns.shape[1]
    total_az = columns.shape[2]
    shaped = columns.reshape(2, row_count, AZ_ROWS, AZ_COLS)
    outer_re, outer_im = dft_table(AZ_ROWS, -1.0)
    inner_re, inner_im = dft_table(AZ_COLS, -1.0)
    twist_index = jnp.arange(AZ_ROWS)[:, None] * jnp.arange(AZ_COLS)[None, :] % total_az
    twist_angle = 2.0 * math.pi / total_az * twist_index.astype(jnp.float32)
    twist_re = jnp.cos(twist_angle)
    twist_im = -jnp.sin(twist_angle)
    section_re, section_im = complex_einsum("ka,cab->ckb", outer_re, outer_im, shaped[0], shaped[1])
    section_re, section_im = (
        section_re * twist_re - section_im * twist_im,
        section_re * twist_im + section_im * twist_re,
    )
    spec_re, spec_im = complex_einsum("ckb,bm->ckm", section_re, section_im, inner_re, inner_im)
    wavenum = jnp.arange(AZ_ROWS)[:, None] + AZ_ROWS * jnp.arange(AZ_COLS)[None, :]
    signed = jnp.where(wavenum < total_az // 2, wavenum, wavenum - total_az).astype(jnp.float32)
    spatial = (2.0 * jnp.pi * signed / total_az) ** 2
    phase_angle = coupling_rows[:, None, None] * spatial[None]
    rot_re = jnp.cos(phase_angle)
    rot_im = -jnp.sin(phase_angle)
    spec_re, spec_im = (spec_re * rot_re - spec_im * rot_im, spec_re * rot_im + spec_im * rot_re)
    back_re, back_im = complex_einsum("ckm,mb->ckb", spec_re, spec_im, inner_re, -inner_im)
    back_re, back_im = (
        back_re * twist_re + back_im * twist_im,
        back_im * twist_re - back_re * twist_im,
    )
    out_re, out_im = complex_einsum("ak,ckb->cab", outer_re, -outer_im, back_re, back_im)
    return jnp.stack([out_re, out_im]).reshape(2, row_count, total_az) / total_az


def local(
    pressure_field,
    block_inverses,
    lower_spikes,
    upper_spikes,
    pade_weights,
    layer_wavenumber,
    layer_index,
    depth_coupling,
    attenuation,
    sediment_type,
):
    block_rows = block_inverses.shape[3]
    layer_onehot = (layer_index[:, None] == jnp.arange(layer_wavenumber.shape[1])[None, :]).astype(
        jnp.float32
    )
    wave_blocks = jnp.dot(layer_onehot, layer_wavenumber.T, precision=FULL_PRECISION)
    wave_rows = jnp.repeat(wave_blocks.T, block_rows, axis=1)
    type_onehot = (jnp.arange(attenuation.shape[1])[:, None] == sediment_type[None, :]).astype(
        jnp.float32
    )
    exponent = jnp.dot(
        jnp.dot(layer_onehot, attenuation, precision=FULL_PRECISION),
        type_onehot,
        precision=FULL_PRECISION,
    )
    damp_rows = jnp.repeat(jnp.exp(-exponent), block_rows, axis=0)
    column_count = pressure_field.shape[1] // lax.axis_size("az")
    coupling_rows = lax.dynamic_slice_in_dim(
        depth_coupling, lax.axis_index("az") * column_count, column_count
    )
    pressure = pressure_field
    for range_step in range(STEPS):
        padded = extended(pressure, (("depth", 1),), 1)
        laplace = padded[:, 2:] + padded[:, :-2] - 2.0 * pressure
        operator_field = jnp.stack(
            [
                laplace[0]
                + wave_rows[0][:, None] * pressure[0]
                - wave_rows[1][:, None] * pressure[1],
                laplace[1]
                + wave_rows[0][:, None] * pressure[1]
                + wave_rows[1][:, None] * pressure[0],
            ]
        )
        columns = lax.all_to_all(
            advance(
                pressure, operator_field, block_inverses, lower_spikes, upper_spikes, pade_weights
            ),
            "az",
            split_axis=1,
            concat_axis=2,
            tiled=True,
        )
        coupled = couple_azimuths(columns, coupling_rows)
        pressure = (
            lax.all_to_all(coupled, "az", split_axis=2, concat_axis=1, tiled=True) * damp_rows[None]
        )
    return pressure


def solution(mesh):
    in_specs = (
        P(None, "depth", "az"),
        P(None, None, "depth", None, None),
        P(None, None, "depth", None),
        P(None, None, "depth", None),
        P(),
        P(),
        P("depth"),
        P("depth"),
        P(),
        P("az"),
    )
    out_specs = P(None, "depth", "az")
    return jax.shard_map(local, mesh=mesh, in_specs=in_specs, out_specs=out_specs, check_vma=False)
```

profile of v0, /device:TPU:11, one launch (start us, length us, event | category | flops | bytes accessed | tf_op | source)
XLA Modules:
  0.0 749.4 jit_solution(16455060894155055137)
XLA Ops:
  49.1 9.6 %fusion.46 = f32[4,512,8,128]{1,2,0,3:T(8,128)} fusion(f32[8,4,128,128]{3,2,1,0:T(8,128)S(1)} %copy-done.22, f32[4,128,512]{2,1,0:T(8,128)S(1)} %get-tuple-element.923), kind=kOutput, calls=%fused_computation.92 | convolution fusion | flops 3221225472 | bytes 11534336 | tf_op jit(solution)/shard_map/tbij,bjn->tbin/dot_general | solution.py:55
  65.9 7.4 subtract_bitcast_fusion.1
  73.5 12.7 %add_bitcast_fusion.1 = f32[8,4,128,512]{3,0,1,2:T(8,128)S(1)} fusion(f32[4,512,8,128]{1,2,0,3:T(8,128)} %fusion.46, f32[8,4,128,128]{3,2,1,0:T(8,128)S(1)} %copy-done.20, f32[4,128,512]{2,1,0:T(8,128)S(1)} %get-tuple-element.924), kind=kOutput, calls=%fused_computation.46 | convolution fusion | flops 3223322624 | bytes 19922944 | tf_op jit(solution)/shard_map/tbij,bjn->tbin/dot_general | solution.py:55
  108.0 14.9 %copy_subtract_fusion.2 = f32[8,4,128,512]{3,2,0,1:T(8,128)} fusion(f32[8,4,128,512]{3,2,0,1:T(8,128)} %copy-done.3, f32[8,4,128,512]{3,0,1,2:T(8,128)} %get-tuple-element.946), kind=kLoop, calls=%fused_computation.37 | loop fusion | flops 2097152 | bytes 25165824 | tf_op jit(solution)/shard_map/sub | solution.py:173
  124.1 18.8 %copy_subtract_fusion.1 = f32[8,4,128,512]{3,2,0,1:T(8,128)} fusion(f32[8,4,128,512]{3,0,1,2:T(8,128)} %get-tuple-element.945, f32[8,4,128,512]{3,0,1,2:T(8,128)} %copy-done.10), kind=kLoop, calls=%fused_computation.36 | loop fusion | flops 2097152 | bytes 25165824 | tf_op jit(solution)/shard_map/sub | solution.py:176
  164.4 23.1 %fusion.16 = (f32[8,4,128,512]{3,2,0,1:T(8,128)}, f32[8,4,128,512]{3,2,0,1:T(8,128)}) fusion(f32[8,4,128,512]{3,2,0,1:T(8,128)} %copy_subtract_fusion.1, f32[8,4,128,512]{3,0,1,2:T(8,128)} %get-tuple-element.957, f32[8,4,128]{2,0,1:T(8,128)S(1)} %copy.192, f32[8,4,512]{2,0,1:T(8,128)S(1)} %pad_maximum_fusion.7, f32[8,4,128,512]{3,2,0,1:T(8,128)} %copy_subtract_fusion.2, ...), kind=kLoop, calls=%fused_computation.33 | loop fusion | flops 12582912 | bytes 50429952 | tf_op jit(solution)/shard_map/sub | solution.py:198
  187.5 15.2 %fusion.28 = f32[1,4,128,512]{3,0,2,1:T(1,128)S(1)} fusion(f32[8,4,128,512]{3,2,0,1:T(8,128)} %get-tuple-element.955, f32[2,8]{1,0:T(2,128)S(1)} %copy-done.24), kind=kOutput, calls=%fused_computation.58 | convolution fusion | flops 25165824 | bytes 9437696 | tf_op jit(solution)/shard_map/t,tbin->bin/dot_general | solution.py:203
  202.8 10.7 %fusion.26 = f32[1,4,128,512]{3,0,2,1:T(1,128)S(1)} fusion(f32[8,4,128,512]{3,2,0,1:T(8,128)S(1)} %copy-done.2, f32[2,8]{1,0:T(2,128)S(1)} %copy-done.24), kind=kOutput, calls=%fused_computation.56 | convolution fusion | flops 25165824 | bytes 9437696 | tf_op jit(solution)/shard_map/t,tbin->bin/dot_general | solution.py:204
  213.5 10.4 %fusion.32 = f32[1,4,128,512]{3,0,2,1:T(1,128)S(1)} fusion(f32[8,4,128,512]{3,2,0,1:T(8,128)S(1)} %bitcast.805, f32[2,8]{1,0:T(2,128)S(1)} %copy-done.24), kind=kOutput, calls=%fused_computation.62 | convolution fusion | flops 25165824 | bytes 9437696 | tf_op jit(solution)/shard_map/t,tbin->bin/dot_general | solution.py:201
  223.9 10.9 %fusion.30 = f32[1,4,128,512]{3,0,2,1:T(1,128)S(1)} fusion(f32[8,4,128,512]{3,2,0,1:T(8,128)S(1)} %bitcast.805, f32[2,8]{1,0:T(2,128)S(1)} %copy-done.24), kind=kOutput, calls=%fused_computation.60 | convolution fusion | flops 25165824 | bytes 9437696 | tf_op jit(solution)/shard_map/t,tbin->bin/dot_general | solution.py:206
  245.3 44.7 %all-to-all-done = f32[2,512,512]{2,0,1:T(2,128)S(1)} async-done(((f32[2,512,512]{2,0,1:T(2,128)}), f32[2,512,512]{2,0,1:T(2,128)S(1)}, u32[]{:S(2)}, u32[]{:S(2)}) %all-to-all-start) | async-done | bytes 2097184 | tf_op jit(solution)/shard_map/all_to_all | solution.py:293
  340.9 7.5 %fusion.397 = f32[4096,2,64]{2,1,0:T(2,128)} fusion(f32[1,64,4096]{1,0,2:T(1,128)S(1)} %bitcast.817, f32[1,64,4096]{1,0,2:T(1,128)} %bitcast.816), kind=kLoop, calls=%fused_computation.599 | loop fusion | flops 1048576 | bytes 4194304
  348.4 8.1 %reshape.3793 = f32[8,1,65536]{2,1,0:T(1,128)} reshape(f32[4096,2,64]{2,1,0:T(2,128)} %fusion.397) | data formatting | bytes 4194304
  363.3 45.4 %all-to-all-done.1 = f32[8,1,65536]{2,1,0:T(1,128)S(1)} async-done(((f32[8,1,65536]{2,1,0:T(1,128)}), f32[8,1,65536]{2,1,0:T(1,128)S(1)}, u32[]{:S(2)}, u32[]{:S(2)}) %all-to-all-start.1) | async-done | bytes 2097184 | tf_op jit(solution)/shard_map/all_to_all | solution.py:304
  410.5 7.4 reduce
  437.3 7.7 %fusion.44 = f32[4,512,8,128]{1,2,0,3:T(8,128)S(1)} fusion(f32[8,4,128,128]{3,2,1,0:T(8,128)S(1)} %copy-done.23, f32[4,128,512]{2,1,0:T(8,128)S(1)} %get-tuple-element.922), kind=kOutput, calls=%fused_computation.90 | convolution fusion | flops 3221225472 | bytes 11534336 | tf_op jit(solution)/shard_map/tbij,bjn->tbin/dot_general | solution.py:52
  444.9 9.5 %fusion.42 = f32[4,512,8,128]{1,2,0,3:T(8,128)} fusion(f32[8,4,128,128]{3,2,1,0:T(8,128)S(1)} %copy-done.23, f32[4,128,512]{2,1,0:T(8,128)S(1)} %get-tuple-element.921), kind=kOutput, calls=%fused_computation.88 | convolution fusion | flops 3221225472 | bytes 11534336 | tf_op jit(solution)/shard_map/tbij,bjn->tbin/dot_general | solution.py:55
  454.5 7.7 %subtract_bitcast_fusion = f32[8,4,128,512]{3,0,1,2:T(8,128)S(1)} fusion(f32[4,512,8,128]{1,2,0,3:T(8,128)S(1)} %fusion.44, f32[8,4,128,128]{3,2,1,0:T(8,128)S(1)} %copy-done.21, f32[4,128,512]{2,1,0:T(8,128)S(1)} %get-tuple-element.921), kind=kOutput, calls=%fused_computation.43 | convolution fusion | flops 3223322624 | bytes 19922944 | tf_op jit(solution)/shard_map/tbij,bjn->tbin/dot_general | solution.py:52
  462.3 12.7 %add_bitcast_fusion = f32[8,4,128,512]{3,0,1,2:T(8,128)S(1)} fusion(f32[4,512,8,128]{1,2,0,3:T(8,128)} %fusion.42, f32[8,4,128,128]{3,2,1,0:T(8,128)S(1)} %copy-done.21, f32[4,128,512]{2,1,0:T(8,128)S(1)} %get-tuple-element.922), kind=kOutput, calls=%fused_computation.42 | convolution fusion | flops 3223322624 | bytes 19922944 | tf_op jit(solution)/shard_map/tbij,bjn->tbin/dot_general | solution.py:55
  543.3 7.8 %fusion.24 = f32[1,4,128,512]{3,0,2,1:T(1,128)S(1)} fusion(f32[8,4,128,512]{3,0,1,2:T(8,128)S(1)} %get-tuple-element.942, f32[2,8]{1,0:T(2,128)S(1)} %copy-done.24), kind=kOutput, calls=%fused_computation.54 | convolution fusion | flops 25165824 | bytes 9437696 | tf_op jit(solution)/shard_map/t,tbin->bin/dot_general | solution.py:201
  561.1 51.6 %all_to_all.66 = f32[2,512,512]{2,0,1:T(2,128)S(1)} all-to-all(f32[2,512,512]{2,0,1:T(2,128)S(1)} %copy.141), channel_id=1, replica_groups=mesh['depth'=4,'az'=8] {'az'}, dimensions={1} | all-to-all | bytes 4194304 | tf_op jit(solution)/shard_map/all_to_all | solution.py:293
  663.5 7.5 %fusion.396 = f32[4096,2,64]{2,1,0:T(2,128)} fusion(f32[1,64,4096]{1,0,2:T(1,128)S(1)} %bitcast.818, f32[1,64,4096]{1,0,2:T(1,128)} %bitcast.815), kind=kLoop, calls=%fused_computation.598 | loop fusion | flops 1048576 | bytes 4194304
  678.1 51.5 %all_to_all.67 = f32[8,1,65536]{2,1,0:T(1,128)} all-to-all(f32[8,1,65536]{2,1,0:T(1,128)S(1)} %reshape.3795), channel_id=1, replica_groups=mesh['depth'=4,'az'=8] {'az'}, dimensions={0} | all-to-all | bytes 4194304 | tf_op jit(solution)/shard_map/all_to_all | solution.py:304
  729.6 7.5 %reduce.1 = f32[8,65536]{1,0:T(8,128)S(1)} reduce(f32[8,1,65536]{2,1,0:T(1,128)} %all_to_all.67, f32[]{:T(128)} %broadcast.1942), dimensions={1}, to_apply=%all_to_all.58.reduce_sub_computation | reduce | bytes 4194308 | tf_op jit(solution)/shard_map/all_to_all | solution.py:304
  (349 shorter events, 344.1 us)
Async XLA Ops:
  0.0 362.9 %copy-start = (f32[5,6]{1,0:T(8,128)S(1)}, f32[5,6]{1,0:T(8,128)}, u32[]{:S(2)}) copy-start(f32[5,6]{1,0:T(8,128)} %param.26) | copy-start | bytes 364
  1.4 45.5 %collective-permute-start = (f32[2,1,512]{2,1,0:T(1,128)}, f32[2,1,512]{2,1,0:T(1,128)}, u32[]{:S(2)}, u32[]{:S(2)}) collective-permute-start(f32[2,1,512]{2,1,0:T(1,128)} %get-tuple-element.939), channel_id=1, source_target_pairs={{8,0},{16,8},{24,16},{9,1},{17,9},{25,17},{10,2},{18,10},{26,18},{... | collective-permute-start | bytes 12296 | tf_op jit(solution)/shard_map/ppermute | solution.py:44
  4.0 42.9 %copy-start.6 = (f32[2,512,512]{2,1,0:T(8,128)S(1)}, f32[2,512,512]{2,1,0:T(8,128)}, u32[]{:S(2)}) copy-start(f32[2,512,512]{2,1,0:T(8,128)} %param.18) | copy-start | bytes 6291460
  4.0 42.9 %collective-permute-start.1 = (f32[2,1,512]{2,1,0:T(1,128)}, f32[2,1,512]{2,1,0:T(1,128)}, u32[]{:S(2)}, u32[]{:S(2)}) collective-permute-start(f32[2,1,512]{2,1,0:T(1,128)} %get-tuple-element.940), channel_id=1, source_target_pairs={{0,8},{8,16},{16,24},{1,9},{9,17},{17,25},{2,10},{10,18},{18,26},{... | collective-permute-start | bytes 12296 | tf_op jit(solution)/shard_map/ppermute | solution.py:42
  12.9 88.0 %copy-start.27 = (f32[8]{0:T(128)}, f32[8]{0:T(128)S(1)}, u32[]{:S(2)}) copy-start(f32[8]{0:T(128)S(1)} %get-tuple-element.982) | copy-start | bytes 100
  17.3 140.5 %copy-start.25 = (f32[8]{0:T(128)}, f32[8]{0:T(128)S(1)}, u32[]{:S(2)}) copy-start(f32[8]{0:T(128)S(1)} %get-tuple-element.979) | copy-start | bytes 100
  73.4 26.9 %copy-start.30 = (f32[4,1,8]{2,1,0:T(1,128)S(1)}, f32[4,1,8]{2,1,0:T(1,128)}, u32[]{:S(2)}) copy-start(f32[4,1,8]{2,1,0:T(1,128)} %all-gather) | copy-start | bytes 388
  73.4 26.9 %copy-start.31 = (f32[4,1,8]{2,1,0:T(1,128)S(1)}, f32[4,1,8]{2,1,0:T(1,128)}, u32[]{:S(2)}) copy-start(f32[4,1,8]{2,1,0:T(1,128)} %all-gather.1) | copy-start | bytes 388
  73.4 27.3 %copy-start.52 = (f32[8]{0:T(128)S(1)}, f32[8]{0:T(128)}, u32[]{:S(2)}) copy-start(f32[8]{0:T(128)} %get-tuple-element.981) | copy-start | bytes 100
  73.4 27.3 %copy-start.54 = (f32[8]{0:T(128)S(1)}, f32[8]{0:T(128)}, u32[]{:S(2)}) copy-start(f32[8]{0:T(128)} %get-tuple-element.985) | copy-start | bytes 100
  73.4 27.5 %copy-start.17 = (f32[1,8,4,128]{1,2,3,0:T(4,128)S(1)}, f32[1,8,4,128]{1,2,3,0:T(4,128)}, u32[]{:S(2)}) copy-start(f32[1,8,4,128]{1,2,3,0:T(4,128)} %copy.184) | copy-start | bytes 49156
  124.0 33.7 %copy-start.50 = (f32[8]{0:T(128)S(1)}, f32[8]{0:T(128)}, u32[]{:S(2)}) copy-start(f32[8]{0:T(128)} %get-tuple-element.973) | copy-start | bytes 100
  124.0 33.7 %copy-start.51 = (f32[8]{0:T(128)S(1)}, f32[8]{0:T(128)}, u32[]{:S(2)}) copy-start(f32[8]{0:T(128)} %get-tuple-element.977) | copy-start | bytes 100
  124.1 33.9 %copy-start.18 = (f32[1,8,4,128]{1,2,3,0:T(4,128)S(1)}, f32[1,8,4,128]{1,2,3,0:T(4,128)}, u32[]{:S(2)}) copy-start(f32[1,8,4,128]{1,2,3,0:T(4,128)} %copy.186) | copy-start | bytes 49156
  124.1 33.9 %copy-start.19 = (f32[1,8,4,128]{1,2,3,0:T(4,128)S(1)}, f32[1,8,4,128]{1,2,3,0:T(4,128)}, u32[]{:S(2)}) copy-start(f32[1,8,4,128]{1,2,3,0:T(4,128)} %copy.187) | copy-start | bytes 49156
  164.4 23.2 %copy-start.24 = (f32[2,8]{1,0:T(2,128)S(1)}, f32[2,8]{1,0:T(2,128)}, u32[]{:S(2)}) copy-start(f32[2,8]{1,0:T(2,128)} %param.22) | copy-start | bytes 196
  187.5 25.9 %slice-start = ((s8[8388608]{0:T(1024)(128)(4,1)}), s8[4194304]{0:T(1024)(128)(4,1)S(1)}, s32[]{:S(2)}) async-start(s8[8388608]{0:T(1024)(128)(4,1)} %bitcast.804), calls=%async_computation.4 | async-start | bytes 8388608
  238.6 51.4 %all-to-all-start = ((f32[2,512,512]{2,0,1:T(2,128)}), f32[2,512,512]{2,0,1:T(2,128)S(1)}, u32[]{:S(2)}, u32[]{:S(2)}) async-start(f32[2,512,512]{2,0,1:T(2,128)} %copy.132), calls=%async_computation | async-start | bytes 4194304 | tf_op jit(solution)/shard_map/all_to_all | solution.py:293
  340.9 22.3 %copy-start.60 = (s32[512]{0:T(512)S(1)}, s32[512]{0:T(512)}, u32[]{:S(2)}) copy-start(s32[512]{0:T(512)} %param.27) | copy-start | bytes 6148
  356.6 52.1 %all-to-all-start.1 = ((f32[8,1,65536]{2,1,0:T(1,128)}), f32[8,1,65536]{2,1,0:T(1,128)S(1)}, u32[]{:S(2)}, u32[]{:S(2)}) async-start(f32[8,1,65536]{2,1,0:T(1,128)} %reshape.3793), calls=%async_computation.1 | async-start | bytes 4194304 | tf_op jit(solution)/shard_map/all_to_all | solution.py:304
  429.7 6.0 collective-permute-start.2
  432.1 3.9 collective-permute-start.3
  462.2 28.0 %copy-start.53 = (f32[8]{0:T(128)S(1)}, f32[8]{0:T(128)}, u32[]{:S(2)}) copy-start(f32[8]{0:T(128)} %get-tuple-element.981) | copy-start | bytes 100
  462.3 28.0 %copy-start.55 = (f32[8]{0:T(128)S(1)}, f32[8]{0:T(128)}, u32[]{:S(2)}) copy-start(f32[8]{0:T(128)} %get-tuple-element.985) | copy-start | bytes 100
  (48 other events, 598.5 us)
where the time goes:
time: 761 us; the launch traced here: 749 us
  matrix products  236 us (31%)
  blocking collectives  166 us (22%)
  other arithmetic  130 us (17%)
  local copies, waits for them, and re-layouts  101 us (13%)
  waiting for transfers between devices  90.4 us (12%)
  starting transfers between devices  23.7 us (3%)
    all_gather x12, blocking collectives, entering_2(): everything = jax.tree.map(lambda part: lax.all_gather(part, axis), value)  63 us
    all_to_all x1, blocking collectives, local(): lax.all_to_all(advance(pressure, operator_field, block_inverses, lower_sp...  51.6 us
    all_to_all x1, blocking collectives, local(): lax.all_to_all(coupled, 'az', split_axis=2, concat_axis=1, tiled=True)  51.5 us
    dot_general x10, matrix products, complex_einsum(): jnp.einsum(formula, left_im, right_re, precision=FULL_PRECISION)  48.1 us
    all_to_all x1, waiting for transfers between devices, local(): lax.all_to_all(coupled, 'az', split_axis=2, concat_axis=1, tiled=True)  45.4 us
    all_to_all x1, waiting for transfers between devices, local(): lax.all_to_all(advance(pressure, operator_field, block_inverses, lower_sp...  44.7 us
    unnamed x146, local copies, waits for them, and re-layouts  44 us
    dot_general x10, matrix products, complex_einsum(): jnp.einsum(formula, left_re, right_im, precision=FULL_PRECISION)  38.9 us
  transfers between devices with their start and end apart: 6, of which 3 were waited for; matrix products, arithmetic and copies ran while one was open for 3% of the time, Pallas kernels for 0%

commit v1 on v0

v1 whole, which is shorter than its diff:
```python
import math

import jax
import jax.numpy as jnp
import numpy as np
from jax import lax
from jax.experimental import pallas as pl
from jax.experimental.pallas import tpu as pltpu
from jax.sharding import PartitionSpec as P

STEPS = 2
LANES = 128
VMEM_BYTES = 48 * 1024 * 1024


def split(value):
    high = value.astype(jnp.bfloat16)
    low = (value - high.astype(jnp.float32)).astype(jnp.bfloat16)
    return high, low


def dot_split(left, right):
    def one(a, b):
        return jnp.dot(a, b, preferred_element_type=jnp.float32)

    return one(left[0], right[0]) + (one(left[0], right[1]) + one(left[1], right[0]))


def mul(a, b):
    return (a[0] * b[0] - a[1] * b[1], a[0] * b[1] + a[1] * b[0])


def sub(a, b):
    return (a[0] - b[0], a[1] - b[1])


def add(a, b):
    return (a[0] + b[0], a[1] + b[1])


def small_dft(values, sign):
    count = len(values)
    if count == 1:
        return values
    even = small_dft(values[0::2], sign)
    odd = small_dft(values[1::2], sign)
    half = count // 2
    low, high = [], []
    for k in range(half):
        re, im = odd[k]
        if k == 0:
            turned = (re, im)
        elif 4 * k == count:
            turned = (-sign * im, sign * re) if sign > 0 else (im, -re)
        elif 8 * k == count:
            root = math.sqrt(0.5)
            turned = ((re - sign * im) * root, (im + sign * re) * root)
        elif 8 * k == 3 * count:
            root = math.sqrt(0.5)
            turned = ((-re - sign * im) * root, (sign * re - im) * root)
        else:
            angle = 2.0 * math.pi * k / count
            turned = mul((re, im), (math.cos(angle), sign * math.sin(angle)))
        low.append(add(even[k], turned))
        high.append(sub(even[k], turned))
    return low + high


def cos_sin(x):
    turns = jnp.floor(x * (2.0 / math.pi) + 0.5)
    r = ((x - turns * 1.5703125) - turns * 4.837512969970703e-4) - turns * 7.549789948768648e-08
    q = turns.astype(jnp.int32)
    s = r * r
    sin_r = r + r * s * (-1.6666654611e-1 + s * (8.3321608736e-3 + s * -1.9515295891e-4))
    cos_r = (1.0 - 0.5 * s) + s * s * (
        4.166664568298827e-2 + s * (-1.388731625493765e-3 + s * 2.443315711809948e-5)
    )
    swap = (q & 1) == 1
    cos_x = jnp.where(swap, sin_r, cos_r)
    sin_x = jnp.where(swap, cos_r, sin_r)
    cos_x = jnp.where(((q + 1) & 2) == 2, -cos_x, cos_x)
    sin_x = jnp.where((q & 2) == 2, -sin_x, sin_x)
    return cos_x, sin_x


def parts8(rows):
    return (rows[0:8], rows[8:16])


def depth_kernel(wave_ref, p_ref, halo_ref, g_ref, col_ref, y_ref, ends_ref, sum_ref):
    blocks, block_rows = g_ref.shape[0], g_ref.shape[2] // 2
    chunk_rows = p_ref.shape[2]
    per = block_rows // chunk_rows
    lane_count = p_ref.shape[3]

    def block_of(part, b):
        return jnp.concatenate([p_ref[b * per + i, part] for i in range(per)], axis=0)

    firsts, lasts = [], []
    for b in range(blocks):
        own = [block_of(0, b), block_of(1, b)]
        lap = []
        for part in range(2):
            if b == 0:
                above = halo_ref[0, part : part + 1]
            else:
                above = p_ref[b * per - 1, part, chunk_rows - 1 : chunk_rows]
            if b == blocks - 1:
                below = halo_ref[1, part : part + 1]
            else:
                below = p_ref[(b + 1) * per, part, 0:1]
            up = jnp.concatenate([above, own[part][:-1]], axis=0)
            down = jnp.concatenate([own[part][1:], below], axis=0)
            lap.append(up + down - 2.0 * own[part])
        w_re, w_im = wave_ref[0, b], wave_ref[1, b]
        x = jnp.concatenate(
            [
                lap[0] + w_re * own[0] - w_im * own[1],
                lap[1] + w_re * own[1] + w_im * own[0],
            ],
            axis=0,
        )
        out = dot_split(split(g_ref[b]), split(x))
        for part in range(2):
            moved = own[part] + out[part * block_rows : (part + 1) * block_rows]
            for i in range(per):
                y_ref[b * per + i, part] = moved[i * chunk_rows : (i + 1) * chunk_rows]
        ends = out[2 * block_rows :]
        ends_ref[b] = ends
        firsts.append(parts8(ends[0:16]))
        lasts.append(parts8(ends[16:32]))
    zero = jnp.zeros((8, lane_count), jnp.float32)
    s = (zero, zero)
    heads = []
    for b in range(blocks):
        heads.append(sub(firsts[b], mul((col_ref[b, 2], col_ref[b, 3]), s)))
        s = sub(lasts[b], mul((col_ref[b, 0], col_ref[b, 1]), s))
    t = (zero, zero)
    for b in reversed(range(blocks)):
        t = sub(heads[b], mul((col_ref[b, 4], col_ref[b, 5]), t))
    sum_ref[...] = jnp.concatenate([s[0], s[1], t[0], t[1]], axis=0)


def link_kernel(here_ref, y_ref, ends_ref, sums_ref, col_ref, c_ref, out_ref):
    blocks = ends_ref.shape[0]
    devices = sums_ref.shape[0]
    chunk_rows = y_ref.shape[2]
    block_rows = c_ref.shape[1] // 2
    per = block_rows // chunk_rows
    here = here_ref[0]
    zero = jnp.zeros((8, y_ref.shape[3]), jnp.float32)

    def lam(b):
        return (col_ref[b, 0], col_ref[b, 1])

    def mu(b):
        return (col_ref[b, 2], col_ref[b, 3])

    def ups(b):
        return (col_ref[b, 4], col_ref[b, 5])

    entering = []
    s = (zero, zero)
    for d in range(devices):
        entering.append(s)
        if d < devices - 1:
            carried = s
            for b in range(d * blocks, (d + 1) * blocks):
                pair = mul(lam(b), carried)
                carried = (-pair[0], -pair[1])
            s = add(carried, parts8(sums_ref[d, 0:16]))
    leaving = [None] * devices
    t = (zero, zero)
    for d in reversed(range(devices)):
        leaving[d] = t
        if d > 0:
            carried = entering[d]
            heads = []
            for b in range(d * blocks, (d + 1) * blocks):
                pair = mul(mu(b), carried)
                heads.append((-pair[0], -pair[1]))
                pair = mul(lam(b), carried)
                carried = (-pair[0], -pair[1])
            back = t
            for b in reversed(range(d * blocks, (d + 1) * blocks)):
                back = sub(heads[b - d * blocks], mul(ups(b), back))
            t = add(back, parts8(sums_ref[d, 16:32]))
    s, t = entering[0], leaving[0]
    for d in range(1, devices):
        s = tuple(jnp.where(here == d, a, b) for a, b in zip(entering[d], s))
        t = tuple(jnp.where(here == d, a, b) for a, b in zip(leaving[d], t))

    def mine(b, k):
        return (col_ref[here * blocks + b, k], col_ref[here * blocks + b, k + 1])

    s_in, heads = [], []
    for b in range(blocks):
        s_in.append(s)
        first, last = parts8(ends_ref[b, 0:16]), parts8(ends_ref[b, 16:32])
        heads.append(sub(first, mul(mine(b, 2), s)))
        s = sub(last, mul(mine(b, 0), s))
    t_in = [None] * blocks
    for b in reversed(range(blocks)):
        t_in[b] = t
        t = sub(heads[b], mul(mine(b, 4), t))
    for b in range(blocks):
        carry = jnp.concatenate([s_in[b][0], s_in[b][1], t_in[b][0], t_in[b][1]], axis=0)
        fix = dot_split(split(c_ref[b]), split(carry))
        for part in range(2):
            for i in range(per):
                low = part * block_rows + i * chunk_rows
                out_ref[b * per + i, part] = y_ref[b * per + i, part] + fix[low : low + chunk_rows]


def azimuth_kernel(
    x_ref, c_ref, spatial_ref, twist_ref, fwd_ref, inv_ref, damp_ref, out_ref, held
):
    sources, rows, lane_count = x_ref.shape[0], x_ref.shape[2], x_ref.shape[3]
    tiles = lane_count // LANES
    outer = sources * tiles

    def where(a):
        return a // tiles, pl.ds((a % tiles) * LANES, LANES)

    @pl.loop(0, rows // 8)
    def _(g):
        at = pl.ds(pl.multiple_of(g * 8, 8), 8)
        values = []
        for a in range(outer):
            src, lanes = where(a)
            values.append((x_ref[src, 0, at, lanes], x_ref[src, 1, at, lanes]))
        for k, value in enumerate(small_dft(values, -1)):
            turned = mul(value, (twist_ref[0, k : k + 1], twist_ref[1, k : k + 1]))
            held[k, at, 0:LANES] = turned[0]
            held[k, at, LANES:] = turned[1]

    fwd = split(fwd_ref[...])
    inv = split(inv_ref[...])
    group = 4

    @pl.loop(0, outer // group)
    def _(g):
        at = pl.ds(g * group, group)
        x = held[at].reshape(group * rows, 2 * LANES)
        spec = dot_split(split(x), fwd).reshape(group, rows, 2 * LANES)
        turn_re, turn_im = cos_sin(c_ref[...][None] * spatial_ref[at])
        re, im = spec[..., :LANES], spec[..., LANES:]
        y = jnp.concatenate([re * turn_re + im * turn_im, im * turn_re - re * turn_im], axis=2)
        held[at] = dot_split(split(y.reshape(group * rows, 2 * LANES)), inv).reshape(
            group, rows, 2 * LANES
        )

    @pl.loop(0, rows // 8)
    def _(g):
        at = pl.ds(pl.multiple_of(g * 8, 8), 8)
        values = []
        for k in range(outer):
            value = (held[k, at, 0:LANES], held[k, at, LANES:])
            values.append(mul(value, (twist_ref[0, k : k + 1], -twist_ref[1, k : k + 1])))
        for a, value in enumerate(small_dft(values, 1)):
            src, lanes = where(a)
            damp = damp_ref[a : a + 1]
            out_ref[src, 0, at, lanes] = value[0] * damp
            out_ref[src, 1, at, lanes] = value[1] * damp


def tables(total):
    outer = total // LANES
    k1 = np.arange(outer)[:, None]
    a2 = np.arange(LANES)[None, :]
    angle = 2.0 * np.pi * ((k1 * a2) % total) / total
    twist = np.stack([np.cos(angle), -np.sin(angle)])
    angle = 2.0 * np.pi * ((np.arange(LANES)[:, None] * a2) % LANES) / LANES
    cos, sin = np.cos(angle), np.sin(angle)
    fwd = np.block([[cos, -sin], [sin, cos]])
    inv = np.block([[cos, sin], [-sin, cos]]) / total
    k = k1 + outer * a2
    signed = np.where(k < total // 2, k, k - total)
    spatial = ((2.0 * np.pi * signed / total) ** 2)[:, None, :]
    return [value.astype(np.float32) for value in (spatial, twist, fwd, inv)]


def vmem(count):
    return [pl.BlockSpec(memory_space=pltpu.VMEM)] * count


def smem():
    return pl.BlockSpec(memory_space=pltpu.SMEM)


def params():
    return pltpu.CompilerParams(vmem_limit_bytes=VMEM_BYTES)


def f32(*shape):
    return jax.ShapeDtypeStruct(shape, jnp.float32)


def weighted(inverses, lower, upper, weights):
    w_re, w_im = weights[0], weights[1]

    def total(re, im):
        shape = (-1,) + (1,) * (re.ndim - 1)
        a, b = w_re.reshape(shape), w_im.reshape(shape)
        return a * re - b * im, a * im + b * re

    m_re, m_im = total(inverses[0], inverses[1])
    m_re, m_im = m_re.sum(0), m_im.sum(0)

    def real_rows(re, im):
        return [jnp.concatenate([re, -im], axis=-1), jnp.concatenate([im, re], axis=-1)]

    first = jnp.moveaxis(inverses[:, :, :, 0], 1, 2)
    last = jnp.moveaxis(inverses[:, :, :, -1], 1, 2)
    g = jnp.concatenate(
        real_rows(m_re, m_im) + real_rows(first[0], first[1]) + real_rows(last[0], last[1]), axis=1
    )
    wl_re, wl_im = (jnp.transpose(v, (1, 2, 0)) for v in total(lower[0], lower[1]))
    wu_re, wu_im = (jnp.transpose(v, (1, 2, 0)) for v in total(upper[0], upper[1]))
    c = jnp.concatenate(
        [
            jnp.concatenate([-wl_re, wl_im, -wu_re, wu_im], axis=-1),
            jnp.concatenate([-wl_im, -wl_re, -wu_im, -wu_re], axis=-1),
        ],
        axis=1,
    )
    return g, c


def local(
    pressure_field,
    block_inverses,
    lower_spikes,
    upper_spikes,
    pade_weights,
    layer_wavenumber,
    layer_index,
    depth_coupling,
    attenuation,
    sediment_type,
):
    parts, depth_rows, az_count = pressure_field.shape
    blocks, block_rows = block_inverses.shape[2], block_inverses.shape[3]
    n_az, n_depth = lax.axis_size("az"), lax.axis_size("depth")
    chunk = depth_rows // n_az
    total = n_az * az_count
    outer = total // LANES
    az_at = lax.axis_index("az")
    spatial, twist, fwd, inv = (jnp.asarray(v) for v in tables(total))
    g, c = weighted(block_inverses, lower_spikes, upper_spikes, pade_weights)
    terms = pade_weights.shape[1]
    columns = jnp.stack(
        [
            lower_spikes[0, :, :, -1],
            lower_spikes[1, :, :, -1],
            lower_spikes[0, :, :, 0],
            lower_spikes[1, :, :, 0],
            upper_spikes[0, :, :, 0],
            upper_spikes[1, :, :, 0],
        ]
    )
    columns = jnp.transpose(columns, (2, 0, 1))
    all_columns = lax.all_gather(columns, "depth").reshape(n_depth * blocks, 6, terms, 1)
    columns = columns.reshape(blocks, 6, terms, 1)
    wave = layer_wavenumber[:, layer_index]
    types = lax.all_gather(sediment_type, "az", tiled=True)
    layer = lax.dynamic_index_in_dim(layer_index, az_at * chunk // block_rows, keepdims=False)
    fade = lax.dynamic_index_in_dim(attenuation, layer, keepdims=False)
    exponent = jnp.zeros(types.shape, jnp.float32)
    for kind in range(attenuation.shape[1]):
        exponent = jnp.where(types == kind, fade[kind], exponent)
    damp = jnp.exp(-exponent).reshape(outer, LANES)
    coupling = lax.dynamic_slice_in_dim(depth_coupling, az_at * chunk, chunk).reshape(chunk, 1)
    here = lax.axis_index("depth").astype(jnp.int32).reshape(1)
    grid_shape = (n_az, parts, chunk, az_count)
    field = jnp.transpose(pressure_field.reshape(parts, n_az, chunk, az_count), (1, 0, 2, 3))
    down = [(i, i + 1) for i in range(n_depth - 1)]
    up = [(i + 1, i) for i in range(n_depth - 1)]
    for _ in range(STEPS):
        halo = jnp.stack(
            [
                lax.ppermute(field[-1, :, -1], "depth", down),
                lax.ppermute(field[0, :, 0], "depth", up),
            ]
        )
        y, ends, sums = pl.pallas_call(
            depth_kernel,
            out_shape=(
                f32(*grid_shape),
                f32(blocks, 4 * terms, az_count),
                f32(4 * terms, az_count),
            ),
            in_specs=[smem()] + vmem(4),
            out_specs=tuple(vmem(3)),
            compiler_params=params(),
            name="depth_solve",
        )(wave, field, halo, g, columns)
        all_sums = lax.all_gather(sums, "depth")
        advanced = pl.pallas_call(
            link_kernel,
            out_shape=f32(*grid_shape),
            in_specs=[smem()] + vmem(5),
            out_specs=vmem(1)[0],
            compiler_params=params(),
            name="depth_link",
        )(here, y, ends, all_sums, all_columns, c)
        lines = lax.all_to_all(advanced, "az", split_axis=0, concat_axis=0, tiled=True)
        coupled = pl.pallas_call(
            azimuth_kernel,
            out_shape=f32(*grid_shape),
            in_specs=vmem(7),
            out_specs=vmem(1)[0],
            scratch_shapes=[pltpu.VMEM((outer, chunk, 2 * LANES), jnp.float32)],
            compiler_params=params(),
            name="azimuth_couple",
        )(lines, coupling, spatial, twist, fwd, inv, damp)
        field = lax.all_to_all(coupled, "az", split_axis=0, concat_axis=0, tiled=True)
    return jnp.transpose(field, (1, 0, 2, 3)).reshape(parts, depth_rows, az_count)


def solution(mesh):
    in_specs = (
        P(None, "depth", "az"),
        P(None, None, "depth", None, None),
        P(None, None, "depth", None),
        P(None, None, "depth", None),
        P(),
        P(),
        P("depth"),
        P("depth"),
        P(),
        P("az"),
    )
    out_specs = P(None, "depth", "az")
    return jax.shard_map(local, mesh=mesh, in_specs=in_specs, out_specs=out_specs, check_vma=False)
```

time: 761 us -> 308 us (0.40)
  matrix products: 236 us -> 0 us
  other arithmetic: 130 us -> 6.93 us
  waiting for transfers between devices: 90.4 us -> 2.41 us
  local copies, waits for them, and re-layouts: 101 us -> 22.2 us
  blocking collectives: 166 us -> 224 us
  Pallas kernels: 0 us -> 23.5 us
    dot_general x51 -> x0, matrix products: 236 us -> none  [the longest x10 48.1 us: complex_einsum(): jnp.einsum(formula, left_im, right_re, precision=FULL_PRECISION)]
    all_to_all x2 -> x1, waiting for transfers between devices: 90.1 us -> 0.01 us  [local(): lax.all_to_all(advanced, 'az', split_axis=0, concat_axis=0, tiled=True)]
    sub x13 -> x0, other arithmetic: 74.9 us -> none  [the longest x2 30.5 us: advance(): swept_im - (upper_re[..., None] * below_im[:, :, None] + upper_im[..., No...]
    all_to_all x2 -> x3, blocking collectives: 103 us -> 153 us  [the longest x2 103 us: local(): lax.all_to_all(coupled, 'az', split_axis=0, concat_axis=0, tiled=True)]
    unnamed x146 -> x64, local copies, waits for them, and re-layouts: 44 us -> 8.71 us
    pallas_call x0 -> x6, Pallas kernels: none -> 23.5 us  [the longest x2 15 us: local(): pl.pallas_call(azimuth_kernel, out_shape=f32(*grid_shape), in_specs=vmem(...]
    unnamed x15 -> x5, other arithmetic: 15.1 us -> 0.09 us
    all_to_all x2 -> x0, other arithmetic: 14.9 us -> none  [local(): lax.all_to_all(coupled, 'az', split_axis=2, concat_axis=1, tiled=True)]
  transfers between devices with their start and end apart: 6 -> 5, of which waited for: 3 -> 1; matrix products, arithmetic and copies ran while one was open for 3% -> 6% of each run, Pallas kernels for 0% -> 0%
where the time goes in v1:
time: 308 us; the launch traced here: 302 us
  blocking collectives  224 us (73%)
  Pallas kernels  23.5 us (8%)
  local copies, waits for them, and re-layouts  22.2 us (7%)
  starting transfers between devices  20.5 us (7%)
  other arithmetic  6.93 us (2%)
    all_to_all x2, blocking collectives, local(): lax.all_to_all(coupled, 'az', split_axis=0, concat_axis=0, tiled=True)  103 us
    all_gather x1, blocking collectives, local(): types = lax.all_gather(sediment_type, 'az', tiled=True)  54.2 us
    all_to_all x1, blocking collectives, local(): lax.all_to_all(advanced, 'az', split_axis=0, concat_axis=0, tiled=True)  50.4 us
    pallas_call x2, Pallas kernels, local(): pl.pallas_call(azimuth_kernel, out_shape=f32(*grid_shape), in_specs=vmem(...  15 us
    all_gather x2, blocking collectives, local(): all_sums = lax.all_gather(sums, 'depth')  10.9 us
    ppermute x2, starting transfers between devices, local(): lax.ppermute(field[-1, :, -1], 'depth', down)  10.6 us
    unnamed x64, local copies, waits for them, and re-layouts  8.71 us
  transfers between devices with their start and end apart: 5, of which 1 were waited for; matrix products, arithmetic and copies ran while one was open for 6% of the time, Pallas kernels for 0%

profile of v1, /device:TPU:11, one launch (start us, length us, event | category | flops | bytes accessed | tf_op | source)
XLA Modules:
  0.0 301.7 jit_solution(10252102802926281841)
XLA Ops:
  0.0 3.4 %copy.101 = f32[2,512,512]{2,0,1:T(2,128)S(1)} copy(f32[2,512,512]{2,1,0:T(8,128)} %param.14) | data formatting | bytes 4194304 | tf_op args[0]
  3.4 3.7 %collective-permute-start = (f32[2,512]{1,0:T(2,128)S(1)}, f32[2,512]{1,0:T(2,128)S(1)}, u32[]{:S(2)}, u32[]{:S(2)}) collective-permute-start(f32[2,512]{1,0:T(2,128)S(1)} %get-tuple-element.30), channel_id=1, source_target_pairs={{0,8},{8,16},{16,24},{1,9},{9,17},{17,25},{2,10},{10,18},{18,26},{... | collective-permute-start | bytes 12296 | tf_op jit(solution)/shard_map/ppermute | solution.py:382
  7.1 1.9 collective-permute-start.1
  11.1 2.0 copy.110.p_ref
  15.0 5.2 %all-gather.1 = f32[16,6,8]{2,1,0:T(8,128)S(1)} all-gather(f32[4,6,8]{2,1,0:T(8,128)S(1)} %copy.112), channel_id=3, replica_groups=mesh['depth'=4,'az'=8] {'depth'}, dimensions={0}, use_global_device_ids=true | all-gather | bytes 3840 | tf_op jit(solution)/shard_map/all_gather | solution.py:363
  21.6 2.4 depth_solve.2
  24.0 6.3 %all-gather = f32[128,512]{1,0:T(8,128)S(1)} all-gather(f32[32,512]{1,0:T(8,128)S(1)} %get-tuple-element.13), channel_id=2, replica_groups=mesh['depth'=4,'az'=8] {'depth'}, dimensions={0}, use_global_device_ids=true | all-gather | bytes 327680 | tf_op jit(solution)/shard_map/all_gather | solution.py:398
  30.3 2.6 depth_link.2
  32.8 5.8 %all-to-all-start = ((f32[8,2,64,512]{3,2,1,0:T(8,128)}), f32[8,2,64,512]{3,2,1,0:T(8,128)S(1)}, u32[]{:S(2)}, u32[]{:S(2)}) async-start(f32[8,2,64,512]{3,2,1,0:T(8,128)} %depth_link.2), calls=%async_computation | async-start | bytes 4194304 | tf_op jit(solution)/shard_map/all_to_all | solution.py:407
  40.6 54.2 %all-gather.3 = s32[8,1,512]{2,1,0:T(1,128)S(1)} all-gather(s32[1,1,512]{2,1,0:T(1,128)S(1)} %bitcast.157), channel_id=1, replica_groups=mesh['depth'=4,'az'=8] {'az'}, dimensions={0}, use_global_device_ids=true | all-gather | bytes 18432 | tf_op jit(solution)/shard_map/all_gather | solution.py:366
  100.1 2.6 compare_select_fusion.2
  102.7 3.2 %exponential_bitcast_fusion.damp_ref = f32[32,128]{1,0:T(8,128)} fusion(pred[4096]{0:T(1024)(128)(4,1)S(1)} %bitcast.147, pred[4096]{0:T(1024)(128)(4,1)S(1)} %bitcast.148, pred[4096]{0:T(1024)(128)(4,1)} %bitcast.149, f32[4096]{0:T(1024)S(1)} %bitcast.144, f32[]{:T(128)} %bitcast.46, f32[]{:T(128)} %bitcast.45, f32[]{:T(128)} %bitcast.44), kind=kLoop, calls=%fused_computation.38 | loop fusion | flops 16384 | bytes 45068 | tf_op jit(solution)/shard_map/reshape | solution.py:372
  109.8 7.5 %azimuth_couple.2 = f32[8,2,64,512]{3,2,1,0:T(8,128)S(1)} custom-call(f32[8,2,64,512]{3,2,1,0:T(8,128)S(1)} %all-to-all-done.x_ref, f32[64,1]{1,0:T(8,128)S(1)} %copy-done.10, f32[32,1,128]{2,1,0:T(1,128)S(1)} %copy-done.16, f32[2,32,128]{2,1,0:T(8,128)S(1)} %copy-done.14, f32[256,256]{1,0:T(8,128)S(1)} %copy-done.5, f32[256,256]{1,0:T(8,128)S(1)} %copy-done.6, ...), custom_call_target="tpu_custom_call" | custom-call | tf_op jit(solution)/shard_map/azimuth_couple/pallas_call | solution.py:408
  117.3 1.6 copy.121
  118.9 52.1 %all_to_all.20 = f32[8,2,64,512]{3,1,2,0:T(2,128)S(1)} all-to-all(f32[8,2,64,512]{3,1,2,0:T(2,128)S(1)} %copy.121), channel_id=1, replica_groups=mesh['depth'=4,'az'=8] {'az'}, dimensions={0} | all-to-all | bytes 4194304 | tf_op jit(solution)/shard_map/all_to_all | solution.py:417
  171.1 6.9 %collective-permute-start.2 = (f32[2,512]{1,0:T(2,128)S(1)}, f32[2,512]{1,0:T(2,128)S(1)}, u32[]{:S(2)}, u32[]{:S(2)}) collective-permute-start(f32[2,512]{1,0:T(2,128)S(1)} %get-tuple-element.28), channel_id=1, source_target_pairs={{0,8},{8,16},{16,24},{1,9},{9,17},{17,25},{2,10},{10,18},{18,26},{... | collective-permute-start | bytes 12296 | tf_op jit(solution)/shard_map/ppermute | solution.py:382
  178.0 2.2 collective-permute-start.3
  180.7 2.4 collective-permute-done.3
  183.1 2.4 depth_solve.3
  185.4 4.6 %all-gather.2 = f32[128,512]{1,0:T(8,128)S(1)} all-gather(f32[32,512]{1,0:T(8,128)S(1)} %get-tuple-element.16), channel_id=4, replica_groups=mesh['depth'=4,'az'=8] {'depth'}, dimensions={0}, use_global_device_ids=true | all-gather | bytes 327680 | tf_op jit(solution)/shard_map/all_gather | solution.py:398
  191.4 50.4 %all_to_all.21.x_ref = f32[8,2,64,512]{3,2,1,0:T(8,128)S(1)} all-to-all(f32[8,2,64,512]{3,2,1,0:T(8,128)S(1)} %depth_link.3), channel_id=1, replica_groups=mesh['depth'=4,'az'=8] {'az'}, dimensions={0} | all-to-all | bytes 4194304 | tf_op jit(solution)/shard_map/all_to_all | solution.py:407
  241.8 7.5 %azimuth_couple.3 = f32[8,2,64,512]{3,2,1,0:T(8,128)S(1)} custom-call(f32[8,2,64,512]{3,2,1,0:T(8,128)S(1)} %all_to_all.21.x_ref, f32[64,1]{1,0:T(8,128)S(1)} %copy-done.11, f32[32,1,128]{2,1,0:T(1,128)S(1)} %copy-done.17, f32[2,32,128]{2,1,0:T(8,128)S(1)} %copy-done.15, f32[256,256]{1,0:T(8,128)S(1)} %copy-done.5, f32[256,256]{1,0:T(8,128)S(1)} %copy-done.7, ...), custom_call_target="tpu_custom_call" | custom-call | tf_op jit(solution)/shard_map/azimuth_couple/pallas_call | solution.py:408
  249.3 50.9 %all_to_all.22 = f32[8,2,64,512]{3,2,1,0:T(8,128)S(1)} all-to-all(f32[8,2,64,512]{3,2,1,0:T(8,128)S(1)} %azimuth_couple.3), channel_id=1, replica_groups=mesh['depth'=4,'az'=8] {'az'}, dimensions={0} | all-to-all | bytes 4194304 | tf_op jit(solution)/shard_map/all_to_all | solution.py:417
  300.2 1.5 copy.127
  (115 shorter events, 16.0 us)
Async XLA Ops:
  0.0 99.4 %copy-start = (f32[5,6]{1,0:T(8,128)S(1)}, f32[5,6]{1,0:T(8,128)}, u32[]{:S(2)}) copy-start(f32[5,6]{1,0:T(8,128)} %param.22) | copy-start | bytes 364
  0.0 9.1 %copy-start.25 = (f32[2,8]{1,0:T(2,128)S(1)}, f32[2,8]{1,0:T(2,128)}, u32[]{:S(2)}) copy-start(f32[2,8]{1,0:T(2,128)} %param.18) | copy-start | bytes 196
  0.0 9.1 %copy-start.20 = (f32[2,8,4,128]{3,2,1,0:T(4,128)S(1)}, f32[2,8,4,128]{3,2,1,0:T(4,128)}, u32[]{:S(2)}) copy-start(f32[2,8,4,128]{3,2,1,0:T(4,128)} %param.16) | copy-start | bytes 98308
  0.0 9.1 %copy-start.22 = (f32[2,8,4,128]{3,2,1,0:T(4,128)S(1)}, f32[2,8,4,128]{3,2,1,0:T(4,128)}, u32[]{:S(2)}) copy-start(f32[2,8,4,128]{3,2,1,0:T(4,128)} %param.17) | copy-start | bytes 98308
  0.0 9.3 %copy-start.19 = (f32[2,8,4,128,128]{4,3,2,1,0:T(8,128)S(1)}, f32[2,8,4,128,128]{4,3,2,1,0:T(8,128)}, u32[]{:S(2)}) copy-start(f32[2,8,4,128,128]{4,3,2,1,0:T(8,128)} %param.15) | copy-start | bytes 12582916
  3.4 6.5 %copy-start.18 = (f32[2,512,512]{2,0,1:T(2,128)}, f32[2,512,512]{2,0,1:T(2,128)S(1)}, u32[]{:S(2)}) copy-start(f32[2,512,512]{2,0,1:T(2,128)S(1)} %copy.101) | copy-start | bytes 6291460
  3.4 18.2 %collective-permute-start = (f32[2,512]{1,0:T(2,128)S(1)}, f32[2,512]{1,0:T(2,128)S(1)}, u32[]{:S(2)}, u32[]{:S(2)}) collective-permute-start(f32[2,512]{1,0:T(2,128)S(1)} %get-tuple-element.30), channel_id=1, source_target_pairs={{0,8},{8,16},{16,24},{1,9},{9,17},{17,25},{2,10},{10,18},{18,26},{... | collective-permute-start | bytes 12296 | tf_op jit(solution)/shard_map/ppermute | solution.py:382
  7.1 14.4 %collective-permute-start.1 = (f32[2,512]{1,0:T(2,128)S(1)}, f32[2,512]{1,0:T(2,128)S(1)}, u32[]{:S(2)}, u32[]{:S(2)}) collective-permute-start(f32[2,512]{1,0:T(2,128)S(1)} %get-tuple-element.31), channel_id=1, source_target_pairs={{8,0},{16,8},{24,16},{9,1},{17,9},{25,17},{10,2},{18,10},{26,18},{... | collective-permute-start | bytes 12296 | tf_op jit(solution)/shard_map/ppermute | solution.py:383
  14.3 16.0 %copy-start.8 = (f32[4,6,8,1]{3,2,1,0:T(8,128)}, f32[4,6,8,1]{3,2,1,0:T(8,128)S(1)}, u32[]{:S(2)}) copy-start(f32[4,6,8,1]{3,2,1,0:T(8,128)S(1)} %copy.111.col_ref) | copy-start | bytes 2308
  21.6 8.7 %copy-start.1 = (f32[4,256,32]{2,1,0:T(8,128)S(1)}, f32[4,256,32]{2,1,0:T(8,128)}, u32[]{:S(2)}) copy-start(f32[4,256,32]{2,1,0:T(8,128)} %copy.119.c_ref) | copy-start | bytes 393220
  21.6 8.7 %copy-start.3 = (f32[16,6,8,1]{3,2,1,0:T(8,128)S(1)}, f32[16,6,8,1]{3,2,1,0:T(8,128)}, u32[]{:S(2)}) copy-start(f32[16,6,8,1]{3,2,1,0:T(8,128)} %copy.118.col_ref) | copy-start | bytes 9220
  32.8 7.7 %copy-start.23 = (s32[512]{0:T(512)S(1)}, s32[512]{0:T(512)}, u32[]{:S(2)}) copy-start(s32[512]{0:T(512)} %param.23) | copy-start | bytes 6148
  32.8 73.1 %copy-start.5 = (f32[256,256]{1,0:T(8,128)S(1)}, f32[256,256]{1,0:T(8,128)}, u32[]{:S(2)}) copy-start(f32[256,256]{1,0:T(8,128)} %constant.62.clone.fwd_ref) | copy-start | bytes 786436
  32.8 73.1 %all-to-all-start = ((f32[8,2,64,512]{3,2,1,0:T(8,128)}), f32[8,2,64,512]{3,2,1,0:T(8,128)S(1)}, u32[]{:S(2)}, u32[]{:S(2)}) async-start(f32[8,2,64,512]{3,2,1,0:T(8,128)} %depth_link.2), calls=%async_computation | async-start | bytes 4194304 | tf_op jit(solution)/shard_map/all_to_all | solution.py:407
  171.1 9.6 %collective-permute-start.2 = (f32[2,512]{1,0:T(2,128)S(1)}, f32[2,512]{1,0:T(2,128)S(1)}, u32[]{:S(2)}, u32[]{:S(2)}) collective-permute-start(f32[2,512]{1,0:T(2,128)S(1)} %get-tuple-element.28), channel_id=1, source_target_pairs={{0,8},{8,16},{16,24},{1,9},{9,17},{17,25},{2,10},{10,18},{18,26},{... | collective-permute-start | bytes 12296 | tf_op jit(solution)/shard_map/ppermute | solution.py:382
  178.0 5.1 %copy-start.9 = (f32[4,6,8,1]{3,2,1,0:T(8,128)S(1)}, f32[4,6,8,1]{3,2,1,0:T(8,128)}, u32[]{:S(2)}) copy-start(f32[4,6,8,1]{3,2,1,0:T(8,128)} %copy-done.8) | copy-start | bytes 2308
  178.0 5.1 %collective-permute-start.3 = (f32[2,512]{1,0:T(2,128)S(1)}, f32[2,512]{1,0:T(2,128)S(1)}, u32[]{:S(2)}, u32[]{:S(2)}) collective-permute-start(f32[2,512]{1,0:T(2,128)S(1)} %get-tuple-element.29), channel_id=1, source_target_pairs={{8,0},{16,8},{24,16},{9,1},{17,9},{25,17},{10,2},{18,10},{26,18},{... | collective-permute-start | bytes 12296 | tf_op jit(solution)/shard_map/ppermute | solution.py:383
  180.6 9.5 %copy-start.2 = (f32[4,256,32]{2,1,0:T(8,128)S(1)}, f32[4,256,32]{2,1,0:T(8,128)}, u32[]{:S(2)}) copy-start(f32[4,256,32]{2,1,0:T(8,128)} %copy.119.c_ref) | copy-start | bytes 393220
  180.6 9.5 %copy-start.4 = (f32[16,6,8,1]{3,2,1,0:T(8,128)S(1)}, f32[16,6,8,1]{3,2,1,0:T(8,128)}, u32[]{:S(2)}) copy-start(f32[16,6,8,1]{3,2,1,0:T(8,128)} %copy.118.col_ref) | copy-start | bytes 9220
  191.3 50.4 %copy-start.7 = (f32[256,256]{1,0:T(8,128)S(1)}, f32[256,256]{1,0:T(8,128)}, u32[]{:S(2)}) copy-start(f32[256,256]{1,0:T(8,128)} %constant.63.clone.inv_ref) | copy-start | bytes 786436
  191.4 50.4 %copy-start.11 = (f32[64,1]{1,0:T(8,128)S(1)}, f32[64,1]{1,0:T(8,128)}, u32[]{:S(2)}) copy-start(f32[64,1]{1,0:T(8,128)} %copy.120.c_ref) | copy-start | bytes 772
  191.4 50.4 %copy-start.13 = (f32[32,128]{1,0:T(8,128)S(1)}, f32[32,128]{1,0:T(8,128)}, u32[]{:S(2)}) copy-start(f32[32,128]{1,0:T(8,128)} %exponential_bitcast_fusion.damp_ref) | copy-start | bytes 49156
  191.4 50.4 %copy-start.15 = (f32[2,32,128]{2,1,0:T(8,128)S(1)}, f32[2,32,128]{2,1,0:T(8,128)}, u32[]{:S(2)}) copy-start(f32[2,32,128]{2,1,0:T(8,128)} %constant.61.clone.twist_ref) | copy-start | bytes 98308
  191.4 50.4 %copy-start.17 = (f32[32,1,128]{2,1,0:T(1,128)S(1)}, f32[32,1,128]{2,1,0:T(1,128)}, u32[]{:S(2)}) copy-start(f32[32,1,128]{2,1,0:T(1,128)} %constant.60.clone.spatial_ref) | copy-start | bytes 49156
  (8 other events, 8.7 us)

commit v2 on v1

--- a/solution.py
+++ b/solution.py
@@ -1,3 +1,4 @@
+import functools
 import math
 
 import jax
@@ -213,7 +214,7 @@
 
 
 def azimuth_kernel(
-    x_ref, c_ref, spatial_ref, twist_ref, fwd_ref, inv_ref, damp_ref, out_ref, held
+    x_ref, c_ref, spatial_ref, twist_ref, fwd_ref, inv_ref, damp_ref, out_ref, edge_ref, held
 ):
     sources, rows, lane_count = x_ref.shape[0], x_ref.shape[2], x_ref.shape[3]
     tiles = lane_count // LANES
@@ -262,6 +263,12 @@
             damp = damp_ref[a : a + 1]
             out_ref[src, 0, at, lanes] = value[0] * damp
             out_ref[src, 1, at, lanes] = value[1] * damp
+
+    for part in range(2):
+        for src in range(sources):
+            row = pl.ds(part * sources + src, 1)
+            edge_ref[0, row] = out_ref[src, part, 0:1]
+            edge_ref[1, row] = out_ref[src, part, rows - 1 : rows]
 
 
 def tables(total):
@@ -278,6 +285,264 @@
     signed = np.where(k < total // 2, k, k - total)
     spatial = ((2.0 * np.pi * signed / total) ** 2)[:, None, :]
     return [value.astype(np.float32) for value in (spatial, twist, fwd, inv)]
+
+
+MESH_IDS = pl.DeviceIdType.MESH
+
+
+def greet(devices):
+    barrier = pltpu.get_barrier_semaphore()
+    for present, device in devices:
+
+        def tell(device=device):
+            pl.semaphore_signal(barrier, inc=1, device_id=device, device_id_type=MESH_IDS)
+
+        if present is None:
+            tell()
+        else:
+            pl.when(present)(tell)
+    amount = 0
+    for present, _ in devices:
+        amount = amount + (1 if present is None else jnp.where(present, 1, 0))
+    pl.semaphore_wait(barrier, amount)
+
+
+def remote(src, dst, send, recv, device):
+    return pltpu.make_async_remote_copy(
+        src_ref=src,
+        dst_ref=dst,
+        send_sem=send,
+        recv_sem=recv,
+        device_id=device,
+        device_id_type=MESH_IDS,
+    )
+
+
+def exchange_kernel(forward, n, src_ref, dst_ref, send_sem, recv_sem):
+    depth, az = lax.axis_index("depth"), lax.axis_index("az")
+    pair, core = depth // 2, depth % 2
+    half = n // 2
+    peers = []
+    for step in range(1, 2 * n):
+        other = (core * n + az + step) % (2 * n)
+        peers.append((None, (2 * pair + other // n, other % n)))
+    greet(peers)
+    moves = []
+    for step in range(n):
+        j = (step + az) % n
+        if forward:
+            device = (2 * pair + j % 2, half * core + j // 2)
+            slot = az
+        else:
+            device = (2 * pair + az // half, j)
+            slot = 2 * (az % half) + core
+        away = jnp.logical_or(device[0] != depth, device[1] != az)
+        move = remote(src_ref.at[j], dst_ref.at[slot], send_sem.at[step], recv_sem.at[slot], device)
+        stay = pltpu.make_async_copy(src_ref.at[j], dst_ref.at[slot], recv_sem.at[slot])
+        pl.when(away)(move.start)
+        pl.when(jnp.logical_not(away))(stay.start)
+        moves.append((away, move))
+    for slot in range(n):
+        pltpu.make_async_copy(src_ref.at[slot], dst_ref.at[slot], recv_sem.at[slot]).wait()
+    for away, move in moves:
+        pl.when(away)(move.wait_send)
+
+
+def exchange(value, forward):
+    n = value.shape[0]
+    return pl.pallas_call(
+        functools.partial(exchange_kernel, forward, n),
+        out_shape=jax.ShapeDtypeStruct(value.shape, value.dtype),
+        in_specs=[pl.BlockSpec(memory_space=pl.ANY)],
+        out_specs=pl.BlockSpec(memory_space=pl.ANY),
+        scratch_shapes=[pltpu.SemaphoreType.DMA((n,)), pltpu.SemaphoreType.DMA((n,))],
+        compiler_params=pltpu.CompilerParams(
+            collective_id=0 if forward else 1, has_side_effects=True
+        ),
+        name="exchange_out" if forward else "exchange_back",
+    )(value)
+
+
+def neighbour_kernel(n, total_blocks, own_ref, edge_ref, other_ref, halo_ref, send_sem, recv_sem):
+    depth, az = lax.axis_index("depth"), lax.axis_index("az")
+    pair, core = depth // 2, depth % 2
+    block = pair * n + az
+    partner = (2 * pair + 1 - core, az)
+    above, below = block > 0, block < total_blocks - 1
+
+    def at(b, c):
+        return (2 * (b // n) + c, b % n)
+
+    greet(
+        [(None, partner)]
+        + [(above, at(block - 1, c)) for c in range(2)]
+        + [(below, at(block + 1, c)) for c in range(2)]
+    )
+    whole = remote(own_ref, other_ref, send_sem.at[0], recv_sem.at[0], partner)
+    whole.start()
+    sends = []
+    for c in range(2):
+        sends.append(
+            (
+                jnp.logical_and(below, core == 1),
+                remote(
+                    edge_ref.at[1], halo_ref.at[0], send_sem.at[1 + c], recv_sem.at[1], at(block + 1, c)
+                ),
+            )
+        )
+        sends.append(
+            (
+                jnp.logical_and(above, core == 0),
+                remote(
+                    edge_ref.at[0], halo_ref.at[1], send_sem.at[3 + c], recv_sem.at[2], at(block - 1, c)
+                ),
+            )
+        )
+    for present, move in sends:
+        pl.when(present)(move.start)
+    for side, present in ((0, above), (1, below)):
+        got = pltpu.make_async_copy(edge_ref.at[side], halo_ref.at[side], recv_sem.at[1 + side])
+        pl.when(present)(got.wait)
+
+        @pl.when(jnp.logical_not(present))
+        def _(side=side):
+            halo_ref[side] = jnp.zeros(halo_ref.shape[1:], jnp.float32)
+
+    for present, move in sends:
+        pl.when(present)(move.wait_send)
+    whole.wait()
+
+
+def neighbours(field, edge, total_blocks):
+    n = field.shape[0]
+    return pl.pallas_call(
+        functools.partial(neighbour_kernel, n, total_blocks),
+        out_shape=(f32(*field.shape), f32(*edge.shape)),
+        in_specs=[pl.BlockSpec(memory_space=pl.ANY), pl.BlockSpec(memory_space=pltpu.VMEM)],
+        out_specs=(pl.BlockSpec(memory_space=pl.ANY), pl.BlockSpec(memory_space=pltpu.VMEM)),
+        scratch_shapes=[pltpu.SemaphoreType.DMA((5,)), pltpu.SemaphoreType.DMA((3,))],
+        compiler_params=pltpu.CompilerParams(collective_id=2, has_side_effects=True),
+        name="neighbours",
+    )(field, edge)
+
+
+def row_solve_kernel(wave_ref, core_ref, own_ref, other_ref, halo_ref, g_ref, y_ref, ends_ref):
+    sources, chunk_rows, lane_count = own_ref.shape[0], own_ref.shape[2], own_ref.shape[3]
+    tiles = lane_count // LANES
+    first = core_ref[0] == 0
+    g = split(g_ref[...])
+    w_re, w_im = wave_ref[0], wave_ref[1]
+    for src in range(sources):
+        own, lap, mine = [], [], []
+        for part in range(2):
+            here, there = own_ref[src, part], other_ref[src, part]
+            top, bottom = jnp.where(first, here, there), jnp.where(first, there, here)
+            row = part * sources + src
+            rows = jnp.concatenate([top, bottom], axis=0)
+            up = jnp.concatenate([halo_ref[0, row : row + 1], rows[:-1]], axis=0)
+            down = jnp.concatenate([rows[1:], halo_ref[1, row : row + 1]], axis=0)
+            own.append(rows)
+            mine.append(here)
+            lap.append(up + down - 2.0 * rows)
+        x = jnp.concatenate(
+            [
+                lap[0] + w_re * own[0] - w_im * own[1],
+                lap[1] + w_re * own[1] + w_im * own[0],
+            ],
+            axis=0,
+        )
+        out = dot_split(g, split(x))
+        y_ref[src, 0] = mine[0] + out[:chunk_rows]
+        y_ref[src, 1] = mine[1] + out[chunk_rows : 2 * chunk_rows]
+        for tile in range(tiles):
+            ends_ref[src * tiles + tile] = out[2 * chunk_rows :, tile * LANES : (tile + 1) * LANES]
+
+
+def sweep_kernel(n, count, ends_ref, col_ref, out_ref, got, answer, sem_a, sem_b, sem_c, sem_d, sem_e):
+    depth, az = lax.axis_index("depth"), lax.axis_index("az")
+    pair, core = depth // 2, depth % 2
+    block = pair * n + az
+    partner = (2 * pair + 1 - core, az)
+
+    def at(b):
+        return (2 * (b // n) + core, b % n)
+
+    others = [(block + step) % count for step in range(1, count)]
+    greet([(None, partner)] + [(None, at(b)) for b in others])
+    base = core * count
+    moves = [
+        remote(ends_ref.at[base + b], got.at[block], sem_a.at[i], sem_b.at[block], at(b))
+        for i, b in enumerate(others)
+    ]
+    for move in moves:
+        move.start()
+    pltpu.make_async_copy(ends_ref.at[base + block], got.at[block], sem_b.at[block]).start()
+    for b in range(count):
+        pltpu.make_async_copy(ends_ref.at[b], got.at[b], sem_b.at[b]).wait()
+    for move in moves:
+        move.wait_send()
+    zero = jnp.zeros((8, LANES), jnp.float32)
+    s = (zero, zero)
+    heads = []
+    for b in range(count):
+        first, last = parts8(got[b, 0:16]), parts8(got[b, 16:32])
+        answer[b, 0:8] = s[0]
+        answer[b, 8:16] = s[1]
+        heads.append(sub(first, mul((col_ref[b, 2], col_ref[b, 3]), s)))
+        s = sub(last, mul((col_ref[b, 0], col_ref[b, 1]), s))
+    t = (zero, zero)
+    for b in reversed(range(count)):
+        answer[b, 16:24] = t[0]
+        answer[b, 24:32] = t[1]
+        t = sub(heads[b], mul((col_ref[b, 4], col_ref[b, 5]), t))
+    moves = [
+        remote(answer.at[b], out_ref.at[base + block], sem_a.at[i], sem_c.at[block], at(b))
+        for i, b in enumerate(others)
+    ]
+    for move in moves:
+        move.start()
+    pltpu.make_async_copy(answer.at[block], out_ref.at[base + block], sem_c.at[block]).start()
+    for b in range(count):
+        pltpu.make_async_copy(answer.at[b], out_ref.at[base + b], sem_c.at[b]).wait()
+    for move in moves:
+        move.wait_send()
+    rows = out_ref.at[pl.ds(base, count)]
+    swap = remote(rows, rows, sem_d.at[0], sem_e.at[0], partner)
+    swap.start()
+    swap.wait()
+
+
+def sweeps(ends, columns, n):
+    count = columns.shape[0]
+    dma = pltpu.SemaphoreType.DMA
+    return pl.pallas_call(
+        functools.partial(sweep_kernel, n, count),
+        out_shape=f32(*ends.shape),
+        in_specs=vmem(2),
+        out_specs=vmem(1)[0],
+        scratch_shapes=[
+            pltpu.VMEM((count, 32, LANES), jnp.float32),
+            pltpu.VMEM((count, 32, LANES), jnp.float32),
+            dma((count - 1,)),
+            dma((count,)),
+            dma((count,)),
+            dma((1,)),
+            dma((1,)),
+        ],
+        compiler_params=pltpu.CompilerParams(collective_id=3, has_side_effects=True),
+        name="sweeps",
+    )(ends, columns)
+
+
+def row_link_kernel(y_ref, carry_ref, c_ref, out_ref):
+    sources, chunk_rows, lane_count = y_ref.shape[0], y_ref.shape[2], y_ref.shape[3]
+    tiles = lane_count // LANES
+    c = split(c_ref[...])
+    for src in range(sources):
+        carry = jnp.concatenate([carry_ref[src * tiles + i] for i in range(tiles)], axis=1)
+        fix = dot_split(c, split(carry))
+        for part in range(2):
+            out_ref[src, part] = y_ref[src, part] + fix[part * chunk_rows : (part + 1) * chunk_rows]
 
 
 def vmem(count):
@@ -364,19 +629,51 @@
     columns = columns.reshape(blocks, 6, terms, 1)
     wave = layer_wavenumber[:, layer_index]
     types = lax.all_gather(sediment_type, "az", tiled=True)
-    layer = lax.dynamic_index_in_dim(layer_index, az_at * chunk // block_rows, keepdims=False)
+    depth_at = lax.axis_index("depth")
+    by_block = (
+        n_az == 2 * blocks
+        and n_depth % 2 == 0
+        and 2 * chunk == block_rows
+        and n_depth * n_az * LANES == total
+    )
+    if by_block:
+        core = depth_at % 2
+        picked = (
+            lax.dynamic_index_in_dim(g, az_at % blocks, keepdims=False),
+            lax.dynamic_index_in_dim(c, az_at % blocks, keepdims=False),
+            lax.dynamic_slice_in_dim(layer_index, az_at % blocks, 1),
+            lax.dynamic_slice_in_dim(depth_coupling, az_at % blocks * block_rows, block_rows),
+        )
+        swap = [(i, i + 1 - 2 * (i % 2)) for i in range(n_depth)]
+        other = jax.tree.map(lambda v: lax.ppermute(v, "depth", swap), picked)
+        mine = core == az_at // blocks
+        g_row, c_row, layer, coupling = jax.tree.map(
+            lambda a, b: jnp.where(mine, a, b), picked, other
+        )
+        layer = layer[0]
+
+        def half(value, start):
+            return lax.dynamic_slice_in_dim(value, start + core * chunk, chunk)
+
+        g_row = jnp.concatenate([half(g_row, 0), half(g_row, block_rows), g_row[2 * block_rows :]])
+        c_row = jnp.concatenate([half(c_row, 0), half(c_row, block_rows)])
+        coupling = half(coupling, 0).reshape(chunk, 1)
+        row_wave = lax.dynamic_index_in_dim(layer_wavenumber, layer, axis=1, keepdims=False)
+    else:
+        layer = lax.dynamic_index_in_dim(layer_index, az_at * chunk // block_rows, keepdims=False)
+        coupling = lax.dynamic_slice_in_dim(depth_coupling, az_at * chunk, chunk).reshape(chunk, 1)
     fade = lax.dynamic_index_in_dim(attenuation, layer, keepdims=False)
     exponent = jnp.zeros(types.shape, jnp.float32)
     for kind in range(attenuation.shape[1]):
         exponent = jnp.where(types == kind, fade[kind], exponent)
     damp = jnp.exp(-exponent).reshape(outer, LANES)
-    coupling = lax.dynamic_slice_in_dim(depth_coupling, az_at * chunk, chunk).reshape(chunk, 1)
     here = lax.axis_index("depth").astype(jnp.int32).reshape(1)
     grid_shape = (n_az, parts, chunk, az_count)
     field = jnp.transpose(pressure_field.reshape(parts, n_az, chunk, az_count), (1, 0, 2, 3))
     down = [(i, i + 1) for i in range(n_depth - 1)]
     up = [(i + 1, i) for i in range(n_depth - 1)]
-    for _ in range(STEPS):
+
+    def slab_solve(field, ready):
         halo = jnp.stack(
             [
                 lax.ppermute(field[-1, :, -1], "depth", down),
@@ -396,6 +693,7 @@
             name="depth_solve",
         )(wave, field, halo, g, columns)
         all_sums = lax.all_gather(sums, "depth")
+        y, ready = lax.optimization_barrier((y, ready))
         advanced = pl.pallas_call(
             link_kernel,
             out_shape=f32(*grid_shape),
@@ -404,17 +702,54 @@
             compiler_params=params(),
             name="depth_link",
         )(here, y, ends, all_sums, all_columns, c)
-        lines = lax.all_to_all(advanced, "az", split_axis=0, concat_axis=0, tiled=True)
-        coupled = pl.pallas_call(
+        return advanced, ready
+
+    def couple(lines):
+        return pl.pallas_call(
             azimuth_kernel,
-            out_shape=f32(*grid_shape),
+            out_shape=(f32(*grid_shape), f32(2, parts * n_az, az_count)),
             in_specs=vmem(7),
-            out_specs=vmem(1)[0],
+            out_specs=tuple(vmem(2)),
             scratch_shapes=[pltpu.VMEM((outer, chunk, 2 * LANES), jnp.float32)],
             compiler_params=params(),
             name="azimuth_couple",
         )(lines, coupling, spatial, twist, fwd, inv, damp)
-        field = lax.all_to_all(coupled, "az", split_axis=0, concat_axis=0, tiled=True)
+
+    def row_solve(field, edge):
+        other, halo = neighbours(field, edge, n_depth * blocks)
+        y, ends = pl.pallas_call(
+            row_solve_kernel,
+            out_shape=(f32(*grid_shape), f32(outer, 4 * terms, LANES)),
+            in_specs=[smem(), smem()] + vmem(4),
+            out_specs=tuple(vmem(2)),
+            compiler_params=params(),
+            name="row_solve",
+        )(row_wave, core.astype(jnp.int32).reshape(1), field, other, halo, g_row)
+        return pl.pallas_call(
+            row_link_kernel,
+            out_shape=f32(*grid_shape),
+            in_specs=vmem(3),
+            out_specs=vmem(1)[0],
+            compiler_params=params(),
+            name="row_link",
+        )(y, sweeps(ends, all_columns, n_az), c_row)
+
+    if by_block:
+        ready = (damp, g_row, c_row, coupling, row_wave)
+        advanced, ready = slab_solve(field, ready)
+        damp, g_row, c_row, coupling, row_wave = ready
+        lines = exchange(advanced, True)
+        for step in range(STEPS):
+            if step:
+                lines = row_solve(lines, edge)
+            lines, edge = couple(lines)
+        field = exchange(lines, False)
+    else:
+        for _ in range(STEPS):
+            advanced, damp = slab_solve(field, damp)
+            lines = lax.all_to_all(advanced, "az", split_axis=0, concat_axis=0, tiled=True)
+            coupled, _ = couple(lines)
+            field = lax.all_to_all(coupled, "az", split_axis=0, concat_axis=0, tiled=True)
     return jnp.transpose(field, (1, 0, 2, 3)).reshape(parts, depth_rows, az_count)
 
 

time: 308 us -> 247 us (0.80); the launches traced: 302 us -> 246 us
  blocking collectives: 224 us -> 36 us
  Pallas kernels: 23.5 us -> 154 us
  starting transfers between devices: 20.5 us -> 6.79 us
  local copies, waits for them, and re-layouts: 22.2 us -> 35 us
  other arithmetic: 6.93 us -> 12.1 us
    all_to_all x3 -> x0, blocking collectives: 153 us -> none  [the longest x2 103 us: local(): lax.all_to_all(coupled, 'az', split_axis=0, concat_axis=0, tiled=True)]
    pallas_call x6 -> x10, Pallas kernels: 23.5 us -> 154 us  [the longest x2 97.8 us: exchange(): pl.pallas_call(functools.partial(exchange_kernel, forward, n), out_shape=...]
    all_gather x1, blocking collectives: 54.2 us -> 19.8 us  [local(): types = lax.all_gather(sediment_type, 'az', tiled=True)]
    ppermute x4 -> x6, starting transfers between devices: 14.8 us -> 6.79 us  [the longest x1 3.52 us: slab_solve(): lax.ppermute(field[-1, :, -1], 'depth', down)]
    unnamed x64 -> x60, local copies, waits for them, and re-layouts: 8.71 us -> 15.5 us
    all_to_all x1 -> x0, starting transfers between devices: 5.78 us -> none  [local(): lax.all_to_all(advanced, 'az', split_axis=0, concat_axis=0, tiled=True)]
    all_gather x1, blocking collectives: 5.16 us -> 10.1 us  [local(): lax.all_gather(columns, 'depth').reshape(n_depth * blocks, 6, terms, 1)]
    all_gather x2 -> x1, blocking collectives: 10.9 us -> 6.05 us  [slab_solve(): all_sums = lax.all_gather(sums, 'depth')]
  transfers between devices with their start and end apart: 5 -> 6, of which waited for: 1 -> 0; matrix products, arithmetic and copies ran while one was open for 6% -> 10% of each run, Pallas kernels for 0% -> 1%
where the time goes in v2:
time: 247 us; the launch traced here: 246 us
  Pallas kernels  154 us (62%)
  blocking collectives  36 us (15%)
  local copies, waits for them, and re-layouts  35 us (14%)
  other arithmetic  12.1 us (5%)
  starting transfers between devices  6.79 us (3%)
    pallas_call x2, Pallas kernels, exchange(): pl.pallas_call(functools.partial(exchange_kernel, forward, n), out_shape=...  97.8 us
    pallas_call x1, Pallas kernels, sweeps(): pl.pallas_call(functools.partial(sweep_kernel, n, count), out_shape=f32(*...  21.7 us
    all_gather x1, blocking collectives, local(): types = lax.all_gather(sediment_type, 'az', tiled=True)  19.8 us
    pallas_call x2, Pallas kernels, couple(): pl.pallas_call(azimuth_kernel, out_shape=(f32(*grid_shape), f32(2, parts...  15.7 us
    unnamed x60, local copies, waits for them, and re-layouts  15.5 us
    all_gather x1, blocking collectives, local(): lax.all_gather(columns, 'depth').reshape(n_depth * blocks, 6, terms, 1)  10.1 us
    pallas_call x1, Pallas kernels, neighbours(): pl.pallas_call(functools.partial(neighbour_kernel, n, total_blocks), out_...  9.74 us
    all_gather x1, blocking collectives, slab_solve(): all_sums = lax.all_gather(sums, 'depth')  6.05 us
  transfers between devices with their start and end apart: 6, of which 0 were waited for; matrix products, arithmetic and copies ran while one was open for 10% of the time, Pallas kernels for 1%

profile of v2, /device:TPU:11, one launch (start us, length us, event | category | flops | bytes accessed | tf_op | source)
XLA Modules:
  0.0 246.0 jit_solution(6493910989707796258)
XLA Ops:
  1.9 2.9 %fusion.1 = (f32[4,128,128]{2,1,0:T(8,128)S(1)}, f32[4,128,128]{2,1,0:T(8,128)S(1)}) fusion(f32[2,8,4,128,128]{4,3,2,1,0:T(8,128)} %param.15, f32[8]{0:T(128)S(1)} %get-tuple-element.73, f32[8]{0:T(128)S(1)} %get-tuple-element.72), kind=kLoop, calls=%fused_computation.4 | loop fusion | flops 4063232 | bytes 4718656 | tf_op jit(solution)/shard_map/reduce_sum | solution.py:573
  8.3 1.3 dynamic_slice.45
  9.7 1.6 copy.93
  13.2 3.5 %collective-permute-start = (f32[2,512]{1,0:T(2,128)}, f32[2,512]{1,0:T(2,128)}, u32[]{:S(2)}, u32[]{:S(2)}) collective-permute-start(f32[2,512]{1,0:T(2,128)} %get-tuple-element.48), channel_id=1, source_target_pairs={{0,8},{8,16},{16,24},{1,9},{9,17},{17,25},{2,10},{10,18},{18,26},{... | collective-permute-start | bytes 12296 | tf_op jit(solution)/shard_map/ppermute | solution.py:679
  17.5 2.0 copy.102.p_ref
  21.0 19.8 %all-gather.2 = s32[8,1,512]{2,1,0:T(1,128)S(1)} all-gather(s32[1,1,512]{2,1,0:T(1,128)S(1)} %bitcast.155), channel_id=1, replica_groups=mesh['depth'=4,'az'=8] {'az'}, dimensions={0}, use_global_device_ids=true | all-gather | bytes 18432 | tf_op jit(solution)/shard_map/all_gather | solution.py:631
  45.9 10.1 %all-gather.1 = f32[16,6,8]{2,1,0:T(8,128)} all-gather(f32[4,6,8]{2,1,0:T(8,128)S(1)} %copy.108), channel_id=3, replica_groups=mesh['depth'=4,'az'=8] {'depth'}, dimensions={0}, use_global_device_ids=true | all-gather | bytes 3840 | tf_op jit(solution)/shard_map/all_gather | solution.py:628
  56.0 2.2 copy.110.col_ref
  58.2 2.1 collective-permute-start.1
  62.2 1.9 compare_select_fusion.2
  64.1 1.9 exponential_bitcast_fusion.damp_ref
  68.4 2.4 depth_solve.1
  70.8 6.0 %all-gather = f32[128,512]{1,0:T(8,128)S(1)} all-gather(f32[32,512]{1,0:T(8,128)S(1)} %get-tuple-element.25), channel_id=2, replica_groups=mesh['depth'=4,'az'=8] {'depth'}, dimensions={0}, use_global_device_ids=true | all-gather | bytes 327680 | tf_op jit(solution)/shard_map/all_gather | solution.py:695
  81.4 48.0 %exchange_out.1.x_ref = f32[8,2,64,512]{3,2,1,0:T(8,128)} custom-call(f32[8,2,64,512]{3,2,1,0:T(8,128)} %copy-done.1), custom_call_target="tpu_custom_call" | custom-call | tf_op jit(solution)/shard_map/exchange_out/pallas_call | solution.py:353
  129.6 1.6 copy-done.4
  131.1 7.5 %azimuth_couple.2 = (f32[8,2,64,512]{3,2,1,0:T(8,128)S(1)}, f32[2,16,512]{2,1,0:T(8,128)S(1)}) custom-call(f32[8,2,64,512]{3,2,1,0:T(8,128)S(1)} %copy-done.4, f32[64,1]{1,0:T(8,128)S(1)} %copy.112.c_ref, f32[32,1,128]{2,1,0:T(1,128)S(1)} %copy-done.16, f32[2,32,128]{2,1,0:T(8,128)S(1)} %copy-done.14, f32[256,256]{1,0:T(8,128)S(1)} %copy-done.11, ...), custom_call_target="tpu_custom_call" | custom-call | tf_op jit(solution)/shard_map/azimuth_couple/pallas_call | solution.py:708
  140.6 9.7 %neighbours.1 = (f32[8,2,64,512]{3,2,1,0:T(8,128)}, f32[2,16,512]{2,1,0:T(8,128)}) custom-call(f32[8,2,64,512]{3,2,1,0:T(8,128)} %copy-done.2, f32[2,16,512]{2,1,0:T(8,128)} %copy-done.17), custom_call_target="tpu_custom_call" | custom-call | tf_op jit(solution)/shard_map/neighbours/pallas_call | solution.py:418
  151.2 4.8 %row_solve.1 = (f32[8,2,64,512]{3,2,1,0:T(8,128)S(1)}, f32[32,32,128]{2,1,0:T(8,128)S(1)}) custom-call(f32[2]{0:T(128)S(1)} %fusion.4.wave_ref, s32[1]{0:T(128)} %bitcast.52.core_ref, f32[8,2,64,512]{3,2,1,0:T(8,128)S(1)} %copy-done.3, f32[8,2,64,512]{3,2,1,0:T(8,128)} %get-tuple-element.30.other_ref, f32[2,16,512]{2,1,0:T(8,128)S(1)} %copy-done.15, ...), custom_call_target="tpu_custom_call" | custom-call | tf_op jit(solution)/shard_map/row_solve/pallas_call | solution.py:720
  158.1 21.7 %sweeps.1.carry_ref = f32[32,32,128]{2,1,0:T(8,128)} custom-call(f32[32,32,128]{2,1,0:T(8,128)} %copy-done.13, f32[16,6,8,1]{3,2,1,0:T(8,128)} %copy.110.col_ref), custom_call_target="tpu_custom_call" | custom-call | tf_op jit(solution)/shard_map/sweeps/pallas_call | solution.py:518
  180.0 1.6 copy-done.8
  183.5 8.2 %azimuth_couple.3 = (f32[8,2,64,512]{3,2,1,0:T(8,128)S(1)}, f32[2,16,512]{2,1,0:T(8,128)}) custom-call(f32[8,2,64,512]{3,2,1,0:T(8,128)S(1)} %row_link.1.x_ref, f32[64,1]{1,0:T(8,128)S(1)} %copy.112.c_ref, f32[32,1,128]{2,1,0:T(1,128)S(1)} %copy-done.16, f32[2,32,128]{2,1,0:T(8,128)S(1)} %copy-done.14, f32[256,256]{1,0:T(8,128)S(1)} %copy-done.11, ...), custom_call_target="tpu_custom_call" | custom-call | tf_op jit(solution)/shard_map/azimuth_couple/pallas_call | solution.py:708
  191.7 1.3 copy-done.9
  193.0 49.8 %exchange_back.1 = f32[8,2,64,512]{3,2,1,0:T(8,128)} custom-call(f32[8,2,64,512]{3,2,1,0:T(8,128)} %copy-done.9), custom_call_target="tpu_custom_call" | custom-call | tf_op jit(solution)/shard_map/exchange_back/pallas_call | solution.py:353
  242.8 3.1 %copy.116 = f32[2,8,64,512]{3,2,1,0:T(8,128)} copy(f32[2,8,64,512]{3,2,0,1:T(8,128)} %bitcast.143) | data formatting | bytes 4194304 | tf_op jit(solution)/shard_map/transpose | solution.py:753
  (122 shorter events, 29.2 us)
Async XLA Ops:
  0.0 61.5 %copy-start = (f32[5,6]{1,0:T(8,128)S(1)}, f32[5,6]{1,0:T(8,128)}, u32[]{:S(2)}) copy-start(f32[5,6]{1,0:T(8,128)} %param.22) | copy-start | bytes 364
  4.8 1.6 copy-start.20
  4.8 1.6 copy-start.21
  4.9 2.4 copy-start.24
  4.9 4.8 %copy-start.19 = (f32[2,512,512]{2,1,0:T(8,128)S(1)}, f32[2,512,512]{2,1,0:T(8,128)}, u32[]{:S(2)}) copy-start(f32[2,512,512]{2,1,0:T(8,128)} %param.14) | copy-start | bytes 6291460
  5.8 72.0 %collective-permute-start.3 = (f32[288,256]{1,0:T(8,128)}, f32[288,256]{1,0:T(8,128)}, u32[]{:S(2)}, u32[]{:S(2)}) collective-permute-start(f32[288,256]{1,0:T(8,128)} %dynamic-slice_bitcast_fusion), channel_id=1, source_target_pairs={{0,8},{8,0},{16,24},{24,16},{1,9},{9,1},{17,25},{25,17},{2,10},{10... | collective-permute-start | bytes 884744 | tf_op jit(solution)/shard_map/ppermute | solution.py:648
  7.3 69.6 %collective-permute-start.4 = (f32[256,32]{0,1:T(8,128)}, f32[256,32]{0,1:T(8,128)}, u32[]{:S(2)}, u32[]{:S(2)}) collective-permute-start(f32[256,32]{0,1:T(8,128)} %dynamic-slice_bitcast_fusion.1), channel_id=1, source_target_pairs={{0,8},{8,0},{16,24},{24,16},{1,9},{9,1},{17,25},{25,17},{2,10},{10... | collective-permute-start | bytes 98312 | tf_op jit(solution)/shard_map/ppermute | solution.py:648
  7.8 50.4 %collective-permute-start.2 = (s32[1]{0:T(128)}, s32[1]{0:T(128)}, u32[]{:S(2)}, u32[]{:S(2)}) collective-permute-start(s32[1]{0:T(128)} %dynamic_slice.37), channel_id=1, source_target_pairs={{0,8},{8,0},{16,24},{24,16},{1,9},{9,1},{17,25},{25,17},{2,10},{10... | collective-permute-start | bytes 20 | tf_op jit(solution)/shard_map/ppermute | solution.py:648
  9.7 57.2 %collective-permute-start.5 = (f32[128]{0:T(128)}, f32[128]{0:T(128)}, u32[]{:S(2)}, u32[]{:S(2)}) collective-permute-start(f32[128]{0:T(128)} %dynamic_slice.45), channel_id=1, source_target_pairs={{0,8},{8,0},{16,24},{24,16},{1,9},{9,1},{17,25},{25,17},{2,10},{10... | collective-permute-start | bytes 1544 | tf_op jit(solution)/shard_map/ppermute | solution.py:648
  11.3 1.3 copy-start.18
  13.2 54.5 %collective-permute-start = (f32[2,512]{1,0:T(2,128)}, f32[2,512]{1,0:T(2,128)}, u32[]{:S(2)}, u32[]{:S(2)}) collective-permute-start(f32[2,512]{1,0:T(2,128)} %get-tuple-element.48), channel_id=1, source_target_pairs={{0,8},{8,16},{16,24},{1,9},{9,17},{17,25},{2,10},{10,18},{18,26},{... | collective-permute-start | bytes 12296 | tf_op jit(solution)/shard_map/ppermute | solution.py:679
  17.5 3.5 %copy-start.23 = (s32[512]{0:T(512)S(1)}, s32[512]{0:T(512)}, u32[]{:S(2)}) copy-start(s32[512]{0:T(512)} %param.23) | copy-start | bytes 6148
  17.5 23.5 %copy-start.22 = (f32[1,8,4,1]{3,2,1,0:T(4,128)S(1)}, f32[1,8,4,1]{3,2,1,0:T(4,128)}, u32[]{:S(2)}) copy-start(f32[1,8,4,1]{3,2,1,0:T(4,128)} %get-tuple-element.63) | copy-start | bytes 388
  58.2 9.5 %collective-permute-start.1 = (f32[2,512]{1,0:T(2,128)}, f32[2,512]{1,0:T(2,128)S(1)}, u32[]{:S(2)}, u32[]{:S(2)}) collective-permute-start(f32[2,512]{1,0:T(2,128)} %get-tuple-element.49), channel_id=1, source_target_pairs={{8,0},{16,8},{24,16},{9,1},{17,9},{25,17},{10,2},{18,10},{26,18},{... | collective-permute-start | bytes 12296 | tf_op jit(solution)/shard_map/ppermute | solution.py:680
  68.4 10.4 %copy-start.5 = (f32[16,6,8,1]{3,2,1,0:T(8,128)S(1)}, f32[16,6,8,1]{3,2,1,0:T(8,128)}, u32[]{:S(2)}) copy-start(f32[16,6,8,1]{3,2,1,0:T(8,128)} %copy.110.col_ref) | copy-start | bytes 9220
  68.4 10.4 %copy-start.6 = (f32[4,256,32]{2,1,0:T(8,128)S(1)}, f32[4,256,32]{2,1,0:T(8,128)}, u32[]{:S(2)}) copy-start(f32[4,256,32]{2,1,0:T(8,128)} %copy.111.c_ref) | copy-start | bytes 393220
  80.1 1.3 copy-start.1
  81.4 48.1 %copy-start.11 = (f32[256,256]{1,0:T(8,128)S(1)}, f32[256,256]{1,0:T(8,128)}, u32[]{:S(2)}) copy-start(f32[256,256]{1,0:T(8,128)} %constant.101.clone.fwd_ref) | copy-start | bytes 786436
  81.4 48.1 %copy-start.12 = (f32[256,256]{1,0:T(8,128)S(1)}, f32[256,256]{1,0:T(8,128)}, u32[]{:S(2)}) copy-start(f32[256,256]{1,0:T(8,128)} %constant.102.clone.inv_ref) | copy-start | bytes 786436
  81.4 48.1 %copy-start.14 = (f32[2,32,128]{2,1,0:T(8,128)S(1)}, f32[2,32,128]{2,1,0:T(8,128)}, u32[]{:S(2)}) copy-start(f32[2,32,128]{2,1,0:T(8,128)} %constant.100.clone.twist_ref) | copy-start | bytes 98308
  81.4 48.1 %copy-start.16 = (f32[32,1,128]{2,1,0:T(1,128)S(1)}, f32[32,1,128]{2,1,0:T(1,128)}, u32[]{:S(2)}) copy-start(f32[32,1,128]{2,1,0:T(1,128)} %constant.99.clone.spatial_ref) | copy-start | bytes 49156
  129.6 1.6 copy-start.4
  140.6 9.8 %copy-start.3 = (f32[8,2,64,512]{3,2,1,0:T(8,128)S(1)}, f32[8,2,64,512]{3,2,1,0:T(8,128)}, u32[]{:S(2)}) copy-start(f32[8,2,64,512]{3,2,1,0:T(8,128)} %copy-done.2) | copy-start | bytes 6291460
  179.9 1.6 copy-start.8
  (7 other events, 7.3 us)

commit v3 on v2

--- a/solution.py
+++ b/solution.py
@@ -260,7 +260,7 @@
             values.append(mul(value, (twist_ref[0, k : k + 1], -twist_ref[1, k : k + 1])))
         for a, value in enumerate(small_dft(values, 1)):
             src, lanes = where(a)
-            damp = damp_ref[a : a + 1]
+            damp = damp_ref[src, 0:1, lanes]
             out_ref[src, 0, at, lanes] = value[0] * damp
             out_ref[src, 1, at, lanes] = value[1] * damp
 
@@ -318,7 +318,9 @@
     )
 
 
-def exchange_kernel(forward, n, src_ref, dst_ref, send_sem, recv_sem):
+def exchange_kernel(forward, n, count, *refs):
+    sources, targets = refs[:count], refs[count : 2 * count]
+    send_sem, recv_sem = refs[2 * count :]
     depth, az = lax.axis_index("depth"), lax.axis_index("az")
     pair, core = depth // 2, depth % 2
     half = n // 2
@@ -337,30 +339,34 @@
             device = (2 * pair + az // half, j)
             slot = 2 * (az % half) + core
         away = jnp.logical_or(device[0] != depth, device[1] != az)
-        move = remote(src_ref.at[j], dst_ref.at[slot], send_sem.at[step], recv_sem.at[slot], device)
-        stay = pltpu.make_async_copy(src_ref.at[j], dst_ref.at[slot], recv_sem.at[slot])
-        pl.when(away)(move.start)
-        pl.when(jnp.logical_not(away))(stay.start)
-        moves.append((away, move))
+        for i, (src_ref, dst_ref) in enumerate(zip(sources, targets)):
+            arrive = recv_sem.at[i, slot]
+            move = remote(src_ref.at[j], dst_ref.at[slot], send_sem.at[i, step], arrive, device)
+            stay = pltpu.make_async_copy(src_ref.at[j], dst_ref.at[slot], arrive)
+            pl.when(away)(move.start)
+            pl.when(jnp.logical_not(away))(stay.start)
+            moves.append((away, move))
     for slot in range(n):
-        pltpu.make_async_copy(src_ref.at[slot], dst_ref.at[slot], recv_sem.at[slot]).wait()
+        for i, (src_ref, dst_ref) in enumerate(zip(sources, targets)):
+            pltpu.make_async_copy(src_ref.at[slot], dst_ref.at[slot], recv_sem.at[i, slot]).wait()
     for away, move in moves:
         pl.when(away)(move.wait_send)
 
 
-def exchange(value, forward):
-    n = value.shape[0]
+def exchange(values, forward):
+    n, count = values[0].shape[0], len(values)
+    anywhere = [pl.BlockSpec(memory_space=pl.ANY)] * count
     return pl.pallas_call(
-        functools.partial(exchange_kernel, forward, n),
-        out_shape=jax.ShapeDtypeStruct(value.shape, value.dtype),
-        in_specs=[pl.BlockSpec(memory_space=pl.ANY)],
-        out_specs=pl.BlockSpec(memory_space=pl.ANY),
-        scratch_shapes=[pltpu.SemaphoreType.DMA((n,)), pltpu.SemaphoreType.DMA((n,))],
+        functools.partial(exchange_kernel, forward, n, count),
+        out_shape=tuple(jax.ShapeDtypeStruct(v.shape, v.dtype) for v in values),
+        in_specs=anywhere,
+        out_specs=tuple(anywhere),
+        scratch_shapes=[pltpu.SemaphoreType.DMA((count, n))] * 2,
         compiler_params=pltpu.CompilerParams(
             collective_id=0 if forward else 1, has_side_effects=True
         ),
         name="exchange_out" if forward else "exchange_back",
-    )(value)
+    )(*values)
 
 
 def neighbour_kernel(n, total_blocks, own_ref, edge_ref, other_ref, halo_ref, send_sem, recv_sem):
@@ -378,8 +384,6 @@
         + [(above, at(block - 1, c)) for c in range(2)]
         + [(below, at(block + 1, c)) for c in range(2)]
     )
-    whole = remote(own_ref, other_ref, send_sem.at[0], recv_sem.at[0], partner)
-    whole.start()
     sends = []
     for c in range(2):
         sends.append(
@@ -400,6 +404,12 @@
         )
     for present, move in sends:
         pl.when(present)(move.start)
+    pieces = [
+        remote(own_ref.at[i], other_ref.at[i], send_sem.at[5 + i], recv_sem.at[3 + i], partner)
+        for i in range(n)
+    ]
+    for piece in pieces:
+        piece.start()
     for side, present in ((0, above), (1, below)):
         got = pltpu.make_async_copy(edge_ref.at[side], halo_ref.at[side], recv_sem.at[1 + side])
         pl.when(present)(got.wait)
@@ -410,7 +420,8 @@
 
     for present, move in sends:
         pl.when(present)(move.wait_send)
-    whole.wait()
+    for piece in pieces:
+        piece.wait()
 
 
 def neighbours(field, edge, total_blocks):
@@ -420,7 +431,7 @@
         out_shape=(f32(*field.shape), f32(*edge.shape)),
         in_specs=[pl.BlockSpec(memory_space=pl.ANY), pl.BlockSpec(memory_space=pltpu.VMEM)],
         out_specs=(pl.BlockSpec(memory_space=pl.ANY), pl.BlockSpec(memory_space=pltpu.VMEM)),
-        scratch_shapes=[pltpu.SemaphoreType.DMA((5,)), pltpu.SemaphoreType.DMA((3,))],
+        scratch_shapes=[pltpu.SemaphoreType.DMA((5 + n,)), pltpu.SemaphoreType.DMA((3 + n,))],
         compiler_params=pltpu.CompilerParams(collective_id=2, has_side_effects=True),
         name="neighbours",
     )(field, edge)
@@ -628,7 +639,6 @@
     all_columns = lax.all_gather(columns, "depth").reshape(n_depth * blocks, 6, terms, 1)
     columns = columns.reshape(blocks, 6, terms, 1)
     wave = layer_wavenumber[:, layer_index]
-    types = lax.all_gather(sediment_type, "az", tiled=True)
     depth_at = lax.axis_index("depth")
     by_block = (
         n_az == 2 * blocks
@@ -662,11 +672,16 @@
     else:
         layer = lax.dynamic_index_in_dim(layer_index, az_at * chunk // block_rows, keepdims=False)
         coupling = lax.dynamic_slice_in_dim(depth_coupling, az_at * chunk, chunk).reshape(chunk, 1)
-    fade = lax.dynamic_index_in_dim(attenuation, layer, keepdims=False)
-    exponent = jnp.zeros(types.shape, jnp.float32)
+    if by_block:
+        types, fade = sediment_type[None], attenuation[layer_index]
+    else:
+        types = lax.all_gather(sediment_type, "az")
+        fade = lax.dynamic_slice_in_dim(attenuation, layer, 1)
+    exponent = jnp.zeros(jnp.broadcast_shapes(types.shape, (fade.shape[0], 1)), jnp.float32)
     for kind in range(attenuation.shape[1]):
-        exponent = jnp.where(types == kind, fade[kind], exponent)
-    damp = jnp.exp(-exponent).reshape(outer, LANES)
+        exponent = jnp.where(types == kind, fade[:, kind : kind + 1], exponent)
+    damp = jnp.exp(-exponent)
+    damp = jnp.repeat(damp, n_az // damp.shape[0], axis=0)[:, None]
     here = lax.axis_index("depth").astype(jnp.int32).reshape(1)
     grid_shape = (n_az, parts, chunk, az_count)
     field = jnp.transpose(pressure_field.reshape(parts, n_az, chunk, az_count), (1, 0, 2, 3))
@@ -738,12 +753,12 @@
         ready = (damp, g_row, c_row, coupling, row_wave)
         advanced, ready = slab_solve(field, ready)
         damp, g_row, c_row, coupling, row_wave = ready
-        lines = exchange(advanced, True)
+        lines, damp = exchange((advanced, damp), True)
         for step in range(STEPS):
             if step:
                 lines = row_solve(lines, edge)
             lines, edge = couple(lines)
-        field = exchange(lines, False)
+        (field,) = exchange((lines,), False)
     else:
         for _ in range(STEPS):
             advanced, damp = slab_solve(field, damp)

time: 247 us -> 223 us (0.903)
  blocking collectives: 36 us -> 10.2 us
  local copies, waits for them, and re-layouts: 35 us -> 39.4 us
  other arithmetic: 12.1 us -> 8.47 us
    all_gather x1 -> x0, blocking collectives: 19.8 us -> none  [local(): types = lax.all_gather(sediment_type, 'az', tiled=True)]
    unnamed x60 -> x63, local copies, waits for them, and re-layouts: 15.5 us -> 21 us
    all_gather x1, blocking collectives: 10.1 us -> 5.02 us  [local(): lax.all_gather(columns, 'depth').reshape(n_depth * blocks, 6, terms, 1)]
  transfers between devices with their start and end apart: 6 -> 6, of which waited for: 0 -> 1; matrix products, arithmetic and copies ran while one was open for 10% -> 10% of each run, Pallas kernels for 1% -> 1%
where the time goes in v3:
time: 223 us; the launch traced here: 222 us
  Pallas kernels  155 us (70%)
  local copies, waits for them, and re-layouts  39.4 us (18%)
  blocking collectives  10.2 us (5%)
  other arithmetic  8.47 us (4%)
  starting transfers between devices  6.79 us (3%)
    pallas_call x2, Pallas kernels, exchange(): pl.pallas_call(functools.partial(exchange_kernel, forward, n, count), out...  98.8 us
    pallas_call x1, Pallas kernels, sweeps(): pl.pallas_call(functools.partial(sweep_kernel, n, count), out_shape=f32(*...  22 us
    unnamed x63, local copies, waits for them, and re-layouts  21 us
    pallas_call x2, Pallas kernels, couple(): pl.pallas_call(azimuth_kernel, out_shape=(f32(*grid_shape), f32(2, parts...  15.6 us
    pallas_call x1, Pallas kernels, neighbours(): pl.pallas_call(functools.partial(neighbour_kernel, n, total_blocks), out_...  9.33 us
    all_gather x1, blocking collectives, slab_solve(): all_sums = lax.all_gather(sums, 'depth')  5.21 us
    all_gather x1, blocking collectives, local(): lax.all_gather(columns, 'depth').reshape(n_depth * blocks, 6, terms, 1)  5.02 us
    pallas_call x1, Pallas kernels, row_solve(): pl.pallas_call(row_solve_kernel, out_shape=(f32(*grid_shape), f32(outer,...  4.56 us
  transfers between devices with their start and end apart: 6, of which 1 were waited for; matrix products, arithmetic and copies ran while one was open for 10% of the time, Pallas kernels for 1%

profile of v3, /device:TPU:11, one launch (start us, length us, event | category | flops | bytes accessed | tf_op | source)
XLA Modules:
  0.0 222.3 jit_solution(9781839283261060375)
XLA Ops:
  1.9 2.9 %fusion.1 = (f32[4,128,128]{2,1,0:T(8,128)S(1)}, f32[4,128,128]{2,1,0:T(8,128)S(1)}) fusion(f32[2,8,4,128,128]{4,3,2,1,0:T(8,128)} %param.15, f32[8]{0:T(128)S(1)} %get-tuple-element.86, f32[8]{0:T(128)S(1)} %get-tuple-element.85), kind=kLoop, calls=%fused_computation.5 | loop fusion | flops 4063232 | bytes 4718656 | tf_op jit(solution)/shard_map/reduce_sum | solution.py:584
  8.4 1.3 dynamic_slice.39
  9.7 4.5 %copy.93 = f32[2,512,512]{2,0,1:T(2,128)} copy(f32[2,512,512]{2,1,0:T(8,128)} %param.14) | data formatting | bytes 4194304 | tf_op args[0]
  15.6 3.5 %collective-permute-start = (f32[2,512]{1,0:T(2,128)}, f32[2,512]{1,0:T(2,128)}, u32[]{:S(2)}, u32[]{:S(2)}) collective-permute-start(f32[2,512]{1,0:T(2,128)} %get-tuple-element.55), channel_id=1, source_target_pairs={{0,8},{8,16},{16,24},{1,9},{9,17},{17,25},{2,10},{10,18},{18,26},{... | collective-permute-start | bytes 12296 | tf_op jit(solution)/shard_map/ppermute | solution.py:694
  19.2 2.0 copy.102.p_ref
  27.3 5.0 %all-gather.1 = f32[16,6,8]{2,1,0:T(8,128)} all-gather(f32[4,6,8]{2,1,0:T(8,128)S(1)} %copy.108), channel_id=3, replica_groups=mesh['depth'=4,'az'=8] {'depth'}, dimensions={0}, use_global_device_ids=true | all-gather | bytes 3840 | tf_op jit(solution)/shard_map/all_gather | solution.py:639
  32.3 2.2 copy.110.col_ref
  34.5 2.1 collective-permute-start.1
  40.3 2.4 %depth_solve.1 = (f32[8,2,64,512]{3,2,1,0:T(8,128)S(1)}, f32[4,32,512]{2,1,0:T(8,128)S(1)}, f32[32,512]{1,0:T(8,128)S(1)}) custom-call(f32[2,4]{1,0:T(2,128)S(1)} %bitcast.124, f32[8,2,64,512]{3,2,1,0:T(8,128)S(1)} %copy.102.p_ref, f32[2,2,512]{2,1,0:T(2,128)S(1)} %pad_maximum_fusion.2.halo_ref, f32[4,288,256]{2,1,0:T(8,128)S(1)} %maximum_dynamic-update-slice_fusion.2.g_ref, ...), custom_call_target="tpu_custom_call" | custom-call | tf_op jit(solution)/shard_map/depth_solve/pallas_call | solution.py:698
  42.7 1.3 copy-done.5
  44.0 5.2 %all-gather = f32[128,512]{1,0:T(8,128)S(1)} all-gather(f32[32,512]{1,0:T(8,128)S(1)} %get-tuple-element.27), channel_id=2, replica_groups=mesh['depth'=4,'az'=8] {'depth'}, dimensions={0}, use_global_device_ids=true | all-gather | bytes 327680 | tf_op jit(solution)/shard_map/all_gather | solution.py:710
  51.4 1.6 copy-done.6
  55.2 1.3 copy-done.1
  56.5 48.9 %exchange_out.1 = (f32[8,2,64,512]{3,2,1,0:T(8,128)}, f32[8,1,512]{2,1,0:T(1,128)}) custom-call(f32[8,2,64,512]{3,2,1,0:T(8,128)} %copy-done.1, f32[8,1,512]{2,1,0:T(1,128)} %broadcast_in_dim_reshape.3.refs_1_), custom_call_target="tpu_custom_call" | custom-call | tf_op jit(solution)/shard_map/exchange_out/pallas_call | solution.py:359
  105.5 1.6 copy-done.11
  107.8 7.4 %azimuth_couple.2 = (f32[8,2,64,512]{3,2,1,0:T(8,128)S(1)}, f32[2,16,512]{2,1,0:T(8,128)S(1)}) custom-call(f32[8,2,64,512]{3,2,1,0:T(8,128)S(1)} %copy-done.11, f32[64,1]{1,0:T(8,128)S(1)} %copy.112.c_ref, f32[32,1,128]{2,1,0:T(1,128)S(1)} %copy-done.20, f32[2,32,128]{2,1,0:T(8,128)S(1)} %copy-done.18, f32[256,256]{1,0:T(8,128)S(1)} %copy-done.13, ...), custom_call_target="tpu_custom_call" | custom-call | tf_op jit(solution)/shard_map/azimuth_couple/pallas_call | solution.py:723
  117.2 9.3 %neighbours.1 = (f32[8,2,64,512]{3,2,1,0:T(8,128)}, f32[2,16,512]{2,1,0:T(8,128)}) custom-call(f32[8,2,64,512]{3,2,1,0:T(8,128)} %copy-done.2, f32[2,16,512]{2,1,0:T(8,128)} %copy-done.23), custom_call_target="tpu_custom_call" | custom-call | tf_op jit(solution)/shard_map/neighbours/pallas_call | solution.py:429
  127.4 4.6 %row_solve.1 = (f32[8,2,64,512]{3,2,1,0:T(8,128)S(1)}, f32[32,32,128]{2,1,0:T(8,128)S(1)}) custom-call(f32[2]{0:T(128)S(1)} %fusion.4.wave_ref, s32[1]{0:T(128)} %bitcast.43.core_ref, f32[8,2,64,512]{3,2,1,0:T(8,128)S(1)} %copy-done.3, f32[8,2,64,512]{3,2,1,0:T(8,128)} %get-tuple-element.34.other_ref, f32[2,16,512]{2,1,0:T(8,128)S(1)} %copy-done.19, ...), custom_call_target="tpu_custom_call" | custom-call | tf_op jit(solution)/shard_map/row_solve/pallas_call | solution.py:735
  134.1 22.0 %sweeps.1.carry_ref = f32[32,32,128]{2,1,0:T(8,128)} custom-call(f32[32,32,128]{2,1,0:T(8,128)} %copy-done.15, f32[16,6,8,1]{3,2,1,0:T(8,128)} %copy.110.col_ref), custom_call_target="tpu_custom_call" | custom-call | tf_op jit(solution)/shard_map/sweeps/pallas_call | solution.py:529
  156.2 1.6 copy-done.9
  159.8 8.1 %azimuth_couple.3 = (f32[8,2,64,512]{3,2,1,0:T(8,128)S(1)}, f32[2,16,512]{2,1,0:T(8,128)}) custom-call(f32[8,2,64,512]{3,2,1,0:T(8,128)S(1)} %row_link.1.x_ref, f32[64,1]{1,0:T(8,128)S(1)} %copy.112.c_ref, f32[32,1,128]{2,1,0:T(1,128)S(1)} %copy-done.20, f32[2,32,128]{2,1,0:T(8,128)S(1)} %copy-done.18, f32[256,256]{1,0:T(8,128)S(1)} %copy-done.13, ...), custom_call_target="tpu_custom_call" | custom-call | tf_op jit(solution)/shard_map/azimuth_couple/pallas_call | solution.py:723
  167.9 1.3 copy-done.10
  169.2 49.9 %exchange_back.1 = f32[8,2,64,512]{3,2,1,0:T(8,128)} custom-call(f32[8,2,64,512]{3,2,1,0:T(8,128)} %copy-done.10), custom_call_target="tpu_custom_call" | custom-call | tf_op jit(solution)/shard_map/exchange_back/pallas_call | solution.py:359
  219.1 3.1 %copy.116 = f32[2,8,64,512]{3,2,1,0:T(8,128)} copy(f32[2,8,64,512]{3,2,0,1:T(8,128)} %bitcast.125) | data formatting | bytes 4194304 | tf_op jit(solution)/shard_map/transpose | solution.py:768
  (125 shorter events, 27.3 us)
Async XLA Ops:
  0.0 25.1 %copy-start = (f32[5,6]{1,0:T(8,128)S(1)}, f32[5,6]{1,0:T(8,128)}, u32[]{:S(2)}) copy-start(f32[5,6]{1,0:T(8,128)} %param.22) | copy-start | bytes 364
  4.8 1.6 copy-start.24
  4.8 1.6 copy-start.25
  4.9 2.4 %copy-start.27 = (s32[4]{0:T(128)S(1)}, s32[4]{0:T(128)}, u32[]{:S(2)}) copy-start(s32[4]{0:T(128)} %param.20) | copy-start | bytes 52
  5.8 44.4 %collective-permute-start.2 = (f32[288,256]{1,0:T(8,128)}, f32[288,256]{1,0:T(8,128)}, u32[]{:S(2)}, u32[]{:S(2)}) collective-permute-start(f32[288,256]{1,0:T(8,128)} %dynamic-slice_bitcast_fusion), channel_id=1, source_target_pairs={{0,8},{8,0},{16,24},{24,16},{1,9},{9,1},{17,25},{25,17},{2,10},{10... | collective-permute-start | bytes 884744 | tf_op jit(solution)/shard_map/ppermute | solution.py:658
  7.3 42.0 %collective-permute-start.3 = (f32[256,32]{0,1:T(8,128)}, f32[256,32]{0,1:T(8,128)}, u32[]{:S(2)}, u32[]{:S(2)}) collective-permute-start(f32[256,32]{0,1:T(8,128)} %dynamic-slice_bitcast_fusion.1), channel_id=1, source_target_pairs={{0,8},{8,0},{16,24},{24,16},{1,9},{9,1},{17,25},{25,17},{2,10},{10... | collective-permute-start | bytes 98312 | tf_op jit(solution)/shard_map/ppermute | solution.py:658
  7.9 26.6 %collective-permute-start.5 = (s32[1]{0:T(128)}, s32[1]{0:T(128)}, u32[]{:S(2)}, u32[]{:S(2)}) collective-permute-start(s32[1]{0:T(128)} %dynamic_slice.41), channel_id=1, source_target_pairs={{0,8},{8,0},{16,24},{24,16},{1,9},{9,1},{17,25},{25,17},{2,10},{10... | collective-permute-start | bytes 20 | tf_op jit(solution)/shard_map/ppermute | solution.py:658
  9.7 28.2 %collective-permute-start.4 = (f32[128]{0:T(128)}, f32[128]{0:T(128)}, u32[]{:S(2)}, u32[]{:S(2)}) collective-permute-start(f32[128]{0:T(128)} %dynamic_slice.39), channel_id=1, source_target_pairs={{0,8},{8,0},{16,24},{24,16},{1,9},{9,1},{17,25},{25,17},{2,10},{10... | collective-permute-start | bytes 1544 | tf_op jit(solution)/shard_map/ppermute | solution.py:658
  15.6 23.2 %collective-permute-start = (f32[2,512]{1,0:T(2,128)}, f32[2,512]{1,0:T(2,128)}, u32[]{:S(2)}, u32[]{:S(2)}) collective-permute-start(f32[2,512]{1,0:T(2,128)} %get-tuple-element.55), channel_id=1, source_target_pairs={{0,8},{8,16},{16,24},{1,9},{9,17},{17,25},{2,10},{10,18},{18,26},{... | collective-permute-start | bytes 12296 | tf_op jit(solution)/shard_map/ppermute | solution.py:694
  19.2 5.1 %copy-start.26 = (f32[2,5]{1,0:T(2,128)S(1)}, f32[2,5]{1,0:T(2,128)}, u32[]{:S(2)}) copy-start(f32[2,5]{1,0:T(2,128)} %param.19) | copy-start | bytes 124
  34.5 5.1 %collective-permute-start.1 = (f32[2,512]{1,0:T(2,128)}, f32[2,512]{1,0:T(2,128)S(1)}, u32[]{:S(2)}, u32[]{:S(2)}) collective-permute-start(f32[2,512]{1,0:T(2,128)} %get-tuple-element.56), channel_id=1, source_target_pairs={{8,0},{16,8},{24,16},{9,1},{17,9},{25,17},{10,2},{18,10},{26,18},{... | collective-permute-start | bytes 12296 | tf_op jit(solution)/shard_map/ppermute | solution.py:695
  42.7 1.3 copy-start.5
  44.0 7.2 %copy-start.16 = (f32[4,32,512]{2,1,0:T(8,128)}, f32[4,32,512]{2,1,0:T(8,128)S(1)}, u32[]{:S(2)}) copy-start(f32[4,32,512]{2,1,0:T(8,128)S(1)} %get-tuple-element.26.ends_ref) | copy-start | bytes 786436
  44.0 7.3 %copy-start.4 = (f32[16,6,8,1]{3,2,1,0:T(8,128)S(1)}, f32[16,6,8,1]{3,2,1,0:T(8,128)}, u32[]{:S(2)}) copy-start(f32[16,6,8,1]{3,2,1,0:T(8,128)} %copy.110.col_ref) | copy-start | bytes 9220
  44.0 7.3 %copy-start.7 = (f32[4,256,32]{2,1,0:T(8,128)S(1)}, f32[4,256,32]{2,1,0:T(8,128)}, u32[]{:S(2)}) copy-start(f32[4,256,32]{2,1,0:T(8,128)} %copy.111.c_ref) | copy-start | bytes 393220
  51.4 1.6 copy-start.6
  55.2 1.3 copy-start.1
  56.5 49.0 %copy-start.13 = (f32[256,256]{1,0:T(8,128)S(1)}, f32[256,256]{1,0:T(8,128)}, u32[]{:S(2)}) copy-start(f32[256,256]{1,0:T(8,128)} %constant.97.clone.fwd_ref) | copy-start | bytes 786436
  56.5 49.0 %copy-start.14 = (f32[256,256]{1,0:T(8,128)S(1)}, f32[256,256]{1,0:T(8,128)}, u32[]{:S(2)}) copy-start(f32[256,256]{1,0:T(8,128)} %constant.98.clone.inv_ref) | copy-start | bytes 786436
  56.5 49.0 %copy-start.18 = (f32[2,32,128]{2,1,0:T(8,128)S(1)}, f32[2,32,128]{2,1,0:T(8,128)}, u32[]{:S(2)}) copy-start(f32[2,32,128]{2,1,0:T(8,128)} %constant.96.clone.twist_ref) | copy-start | bytes 98308
  56.5 49.0 %copy-start.20 = (f32[32,1,128]{2,1,0:T(1,128)S(1)}, f32[32,1,128]{2,1,0:T(1,128)}, u32[]{:S(2)}) copy-start(f32[32,1,128]{2,1,0:T(1,128)} %constant.95.clone.spatial_ref) | copy-start | bytes 49156
  105.5 1.6 copy-start.11
  117.2 9.3 %copy-start.3 = (f32[8,2,64,512]{3,2,1,0:T(8,128)S(1)}, f32[8,2,64,512]{3,2,1,0:T(8,128)}, u32[]{:S(2)}) copy-start(f32[8,2,64,512]{3,2,1,0:T(8,128)} %copy-done.2) | copy-start | bytes 6291460
  156.2 1.6 copy-start.9
  (10 other events, 9.9 us)
